TPU v7x, 256 devices: a whole 4x4x8 slice. The times are simulated.
256 devices in a mesh: ctx: 128 (over x_hi, z, y, core), ch: 2 (over x_lo).
Axes of the slice: x: 4 (x_hi: 2, x_lo: 2; x = x_hi * 2 + x_lo), y: 4, z: 8, core: 2. Of those that a mesh axis runs over, the one named last changes fastest.
Arguments:
- query_proj: bfloat16 [128, 32768], P('ch', 'ctx'), may hold values from -6 to 6
- key_proj: bfloat16 [128, 32768], P('ch', 'ctx'), may hold values from -6 to 6
- value_proj: bfloat16 [128, 32768], P('ch', 'ctx'), may hold values from -6 to 6
- filter_taps: float32 [32768], P('ctx'), may hold values from -0.03125 to 0.03125
- out_grad: bfloat16 [128, 32768], P('ch', 'ctx'), may hold values from -6 to 6
Outputs:
- query_grad: bfloat16 [128, 32768], P('ch', 'ctx')
- key_grad: bfloat16 [128, 32768], P('ch', 'ctx')
- value_grad: bfloat16 [128, 32768], P('ch', 'ctx')
- filter_grad: float32 [32768], P('ctx')
All inputs are finite; a program needn't handle non-finite values.
Results may differ from a plain program's by a relative error of at most 0.0033.
Values sent between devices are 32-bit elements; how exact they have to be, the bound alone decides.
No kernel may reach another device: no remote copies, remote signals or barrier semaphores. Data moves between devices by JAX's collectives and lax.ppermute only.
A program may use at most 64 MiB of HBM per device.

v0:
```python
import math

import jax
import jax.numpy as jnp
from jax import lax
from jax.sharding import PartitionSpec as P


def contract(pattern, former, latter):
    return jnp.einsum(
        pattern, former, latter, precision=lax.Precision.HIGHEST, preferred_element_type=jnp.float32
    )


def phase_of(product, period):
    angles = (product % period).astype(jnp.float32) * (2.0 * math.pi / period)
    return (jnp.cos(angles), jnp.sin(angles))


def grid_table(first, second, period):
    row_index = lax.broadcasted_iota(jnp.int32, (first, second), 0)
    column_index = lax.broadcasted_iota(jnp.int32, (first, second), 1)
    return phase_of(row_index * column_index, period)


def forward_front(signal, small_cosine, small_sine, twist_cosine, twist_sine):
    real_part = contract("rsn,nk->rsk", signal, small_cosine)
    imaginary = -contract("rsn,nk->rsk", signal, small_sine)
    return (
        real_part * twist_cosine + imaginary * twist_sine,
        imaginary * twist_cosine - real_part * twist_sine,
    )


def forward_back(real_part, imaginary, inner_cosine, inner_sine):
    row_count, stripes, double = real_part.shape
    real_grid = real_part.reshape(row_count, stripes, double // 2, 2)
    imag_grid = imaginary.reshape(row_count, stripes, double // 2, 2)
    spec_real = contract("rsjq,sjm->rqm", real_grid, inner_cosine) + contract(
        "rsjq,sjm->rqm", imag_grid, inner_sine
    )
    spec_imag = contract("rsjq,sjm->rqm", imag_grid, inner_cosine) - contract(
        "rsjq,sjm->rqm", real_grid, inner_sine
    )
    return (spec_real, spec_imag)


def inverse_front(real_part, imaginary, inner_cosine, inner_sine, twist_cosine, twist_sine):
    row_count = real_part.shape[0]
    stripes = inner_cosine.shape[0]
    wave_real = contract("rqm,sjm->rsjq", real_part, inner_cosine) - contract(
        "rqm,sjm->rsjq", imaginary, inner_sine
    )
    wave_imag = contract("rqm,sjm->rsjq", real_part, inner_sine) + contract(
        "rqm,sjm->rsjq", imaginary, inner_cosine
    )
    turned_real = wave_real * twist_cosine - wave_imag * twist_sine
    turned_imag = wave_real * twist_sine + wave_imag * twist_cosine
    return (
        turned_real.reshape(row_count, stripes, -1),
        turned_imag.reshape(row_count, stripes, -1),
    )


def inverse_back(real_part, imaginary, outer_cosine, outer_sine, factor):
    values_real = (
        contract("rsk,kn->rsn", real_part, outer_cosine)
        - contract("rsk,kn->rsn", imaginary, outer_sine)
    ) * factor
    return (values_real, values_real)


def shards(query_proj, key_proj, value_proj, filter_taps, out_grad):
    groups = lax.axis_size("ctx")
    owner = lax.axis_index("ctx")
    channels, length = query_proj.shape
    stripes = length // groups
    padded = 2 * groups * length
    factor = 1.0 / padded
    inner_cosine, inner_sine = grid_table(length, length, length)
    inner_cosine = inner_cosine.reshape(stripes, groups, length)
    inner_sine = inner_sine.reshape(stripes, groups, length)
    small_cosine, small_sine = grid_table(groups, 2 * groups, 2 * groups)
    outer_cosine, outer_sine = grid_table(2 * groups, groups, 2 * groups)
    offsets = lax.broadcasted_iota(jnp.int32, (stripes, 2 * groups), 0) * groups + owner
    frequency = lax.broadcasted_iota(jnp.int32, (stripes, 2 * groups), 1)
    ahead_cosine, ahead_sine = phase_of(offsets * frequency, padded)
    places = lax.broadcasted_iota(
        jnp.int32, (stripes, groups, 2), 0
    ) * groups + lax.broadcasted_iota(jnp.int32, (stripes, groups, 2), 1)
    owned_bins = 2 * owner + lax.broadcasted_iota(jnp.int32, (stripes, groups, 2), 2)
    return_cosine, return_sine = phase_of(places * owned_bins, padded)
    gated = key_proj.astype(jnp.float32) * value_proj.astype(jnp.float32)
    gate_grad = out_grad.astype(jnp.float32) * query_proj.astype(jnp.float32)
    taps = filter_taps.reshape(1, length)

    def transform(signal):
        columns = lax.all_to_all(
            signal.reshape(signal.shape[0], stripes, groups),
            "ctx",
            split_axis=2,
            concat_axis=2,
            tiled=True,
        )
        front_real, front_imag = forward_front(
            columns, small_cosine, small_sine, ahead_cosine, ahead_sine
        )
        moved_real, moved_imag = (
            lax.all_to_all(front_real, "ctx", split_axis=2, concat_axis=2, tiled=True),
            lax.all_to_all(front_imag, "ctx", split_axis=2, concat_axis=2, tiled=True),
        )
        return forward_back(moved_real, moved_imag, inner_cosine, inner_sine)

    gated_real, gated_imag = transform(gated)
    grad_real, grad_imag = transform(gate_grad)
    taps_real, taps_imag = transform(taps)
    cross_real = jnp.sum(grad_real * gated_real + grad_imag * gated_imag, axis=0, keepdims=True)
    cross_imag = jnp.sum(grad_imag * gated_real - grad_real * gated_imag, axis=0, keepdims=True)
    cross_real, cross_imag = lax.psum((cross_real, cross_imag), "ch")
    conv_real = gated_real * taps_real - gated_imag * taps_imag
    conv_imag = gated_real * taps_imag + gated_imag * taps_real
    back_real = grad_real * taps_real + grad_imag * taps_imag
    back_imag = grad_imag * taps_real - grad_real * taps_imag

    def restore(real_part, imaginary):
        row_count = real_part.shape[0]
        turned_real, turned_imag = inverse_front(
            real_part, imaginary, inner_cosine, inner_sine, return_cosine, return_sine
        )
        here_real, here_imag = (
            lax.all_to_all(turned_real, "ctx", split_axis=2, concat_axis=2, tiled=True),
            lax.all_to_all(turned_imag, "ctx", split_axis=2, concat_axis=2, tiled=True),
        )
        values, unused = inverse_back(here_real, here_imag, outer_cosine, outer_sine, factor)
        placed = lax.all_to_all(values, "ctx", split_axis=2, concat_axis=2, tiled=True)
        return placed.reshape(row_count, length)

    conv_out = restore(conv_real, conv_imag)
    back_out = restore(back_real, back_imag)
    filter_out = restore(cross_real, cross_imag)[0]
    query_grad = (out_grad.astype(jnp.float32) * conv_out).astype(jnp.bfloat16)
    key_grad = (back_out * value_proj.astype(jnp.float32)).astype(jnp.bfloat16)
    value_grad = (back_out * key_proj.astype(jnp.float32)).astype(jnp.bfloat16)
    total_channels = channels * lax.axis_size("ch")
    filter_grad = filter_out * (1.0 / math.sqrt(total_channels * length * groups))
    return (query_grad, key_grad, value_grad, filter_grad)


def solution(mesh):
    placed = (P("ch", "ctx"), P("ch", "ctx"), P("ch", "ctx"), P("ctx"), P("ch", "ctx"))
    return jax.shard_map(
        shards,
        mesh=mesh,
        in_specs=placed,
        out_specs=(P("ch", "ctx"), P("ch", "ctx"), P("ch", "ctx"), P("ctx")),
        check_vma=False,
    )
```

profile of v0, /device:TPU:1, one launch (start us, length us, event | category | flops | bytes accessed | tf_op | source)
XLA Modules:
  0.0 410.5 jit_solution(18212417500371747862)
XLA Ops:
  2.0 16.5 %all-to-all-start.3 = ((f32[1,2,128]{1,0,2:T(1,128)}), f32[1,2,128]{1,0,2:T(1,128)S(1)}, u32[]{:S(2)}, u32[]{:S(2)}) async-start(f32[1,2,128]{1,0,2:T(1,128)} %copy.164), calls=%async_computation.3 | async-start | bytes 131072 | tf_op jit(solution)/shard_map/all_to_all | solution.py:98
  18.7 12.3 %all-to-all-done.3 = f32[1,2,128]{1,0,2:T(1,128)S(1)} async-done(((f32[1,2,128]{1,0,2:T(1,128)}), f32[1,2,128]{1,0,2:T(1,128)S(1)}, u32[]{:S(2)}, u32[]{:S(2)}) %all-to-all-start.3) | async-done | bytes 1056 | tf_op jit(solution)/shard_map/all_to_all | solution.py:98
  33.1 5.8 %all-to-all-start.5 = ((f32[1,2,256]{1,0,2:T(1,128)}), f32[1,2,256]{1,0,2:T(1,128)S(1)}, u32[]{:S(2)}, u32[]{:S(2)}) async-start(f32[1,2,256]{1,0,2:T(1,128)} %copy.168), calls=%async_computation.5 | async-start | bytes 262144 | tf_op jit(solution)/shard_map/all_to_all | solution.py:110
  39.8 13.1 %all-to-all-done.5 = f32[1,2,256]{1,0,2:T(1,128)S(1)} async-done(((f32[1,2,256]{1,0,2:T(1,128)}), f32[1,2,256]{1,0,2:T(1,128)S(1)}, u32[]{:S(2)}, u32[]{:S(2)}) %all-to-all-start.5) | async-done | bytes 2080 | tf_op jit(solution)/shard_map/all_to_all | solution.py:110
  52.9 5.5 %all-to-all-start.4 = ((f32[1,2,256]{1,0,2:T(1,128)}), f32[1,2,256]{1,0,2:T(1,128)S(1)}, u32[]{:S(2)}, u32[]{:S(2)}) async-start(f32[1,2,256]{1,0,2:T(1,128)} %copy.165), calls=%async_computation.4 | async-start | bytes 262144 | tf_op jit(solution)/shard_map/all_to_all | solution.py:109
  60.3 12.2 %all-to-all-done.4 = f32[1,2,256]{1,0,2:T(1,128)S(1)} async-done(((f32[1,2,256]{1,0,2:T(1,128)}), f32[1,2,256]{1,0,2:T(1,128)S(1)}, u32[]{:S(2)}, u32[]{:S(2)}) %all-to-all-start.4) | async-done | bytes 2080 | tf_op jit(solution)/shard_map/all_to_all | solution.py:109
  72.5 5.8 %all-to-all-start.9 = ((f32[128,1,128]{2,1,0:T(1,128)}), f32[128,1,128]{2,1,0:T(1,128)S(1)}, u32[]{:S(2)}, u32[]{:S(2)}) async-start(f32[128,1,128]{2,1,0:T(1,128)} %reshape.338), calls=%async_computation.9 | async-start | bytes 131072 | tf_op jit(solution)/shard_map/all_to_all | solution.py:98
  79.3 1.2 convolution_bitcast_fusion.10
  80.5 10.2 %all-to-all-done.9 = f32[128,1,128]{2,1,0:T(1,128)S(1)} async-done(((f32[128,1,128]{2,1,0:T(1,128)}), f32[128,1,128]{2,1,0:T(1,128)S(1)}, u32[]{:S(2)}, u32[]{:S(2)}) %all-to-all-start.9) | async-done | bytes 65568 | tf_op jit(solution)/shard_map/all_to_all | solution.py:98
  94.9 5.8 %all-to-all-start.11 = ((f32[128,1,256]{2,1,0:T(1,128)}), f32[128,1,256]{2,1,0:T(1,128)S(1)}, u32[]{:S(2)}, u32[]{:S(2)}) async-start(f32[128,1,256]{2,1,0:T(1,128)} %reshape.342), calls=%async_computation.11 | async-start | bytes 262144 | tf_op jit(solution)/shard_map/all_to_all | solution.py:110
  100.7 1.2 convolution_bitcast_fusion.8
  101.9 1.3 fusion.6
  104.3 10.4 %all-to-all-done.11 = f32[128,1,256]{2,1,0:T(1,128)S(1)} async-done(((f32[128,1,256]{2,1,0:T(1,128)}), f32[128,1,256]{2,1,0:T(1,128)S(1)}, u32[]{:S(2)}, u32[]{:S(2)}) %all-to-all-start.11) | async-done | bytes 131104 | tf_op jit(solution)/shard_map/all_to_all | solution.py:110
  114.7 6.1 %all-to-all-start.10 = ((f32[128,1,256]{2,1,0:T(1,128)}), f32[128,1,256]{2,1,0:T(1,128)S(1)}, u32[]{:S(2)}, u32[]{:S(2)}) async-start(f32[128,1,256]{2,1,0:T(1,128)} %reshape.340), calls=%async_computation.10 | async-start | bytes 262144 | tf_op jit(solution)/shard_map/all_to_all | solution.py:109
  120.8 1.2 fusion.7
  122.0 1.0 reduce.1
  123.4 1.3 convolution_bitcast_fusion.2
  124.7 10.0 %all-to-all-done.10 = f32[128,1,256]{2,1,0:T(1,128)S(1)} async-done(((f32[128,1,256]{2,1,0:T(1,128)}), f32[128,1,256]{2,1,0:T(1,128)S(1)}, u32[]{:S(2)}, u32[]{:S(2)}) %all-to-all-start.10) | async-done | bytes 131104 | tf_op jit(solution)/shard_map/all_to_all | solution.py:109
  134.7 1.0 reduce.2
  136.0 1.3 convolution_bitcast_fusion
  137.3 1.3 fusion.2
  138.7 1.3 fusion.3
  140.0 1.7 fusion.29
  141.7 1.7 fusion.24
  143.4 1.7 convolution_add_fusion
  145.1 1.7 add_bitcast_fusion
  148.2 5.7 %all-to-all-start.13 = ((f32[128,1,256]{2,1,0:T(1,128)}), f32[128,1,256]{2,1,0:T(1,128)S(1)}, u32[]{:S(2)}, u32[]{:S(2)}) async-start(f32[128,1,256]{2,1,0:T(1,128)} %reshape.346), calls=%async_computation.13 | async-start | bytes 262144 | tf_op jit(solution)/shard_map/all_to_all | solution.py:132
  155.2 12.8 %all-to-all-done.13 = f32[128,1,256]{2,1,0:T(1,128)S(1)} async-done(((f32[128,1,256]{2,1,0:T(1,128)}), f32[128,1,256]{2,1,0:T(1,128)S(1)}, u32[]{:S(2)}, u32[]{:S(2)}) %all-to-all-start.13) | async-done | bytes 131104 | tf_op jit(solution)/shard_map/all_to_all | solution.py:132
  167.9 5.5 %all-to-all-start.12 = ((f32[128,1,256]{2,1,0:T(1,128)}), f32[128,1,256]{2,1,0:T(1,128)S(1)}, u32[]{:S(2)}, u32[]{:S(2)}) async-start(f32[128,1,256]{2,1,0:T(1,128)} %reshape.344), calls=%async_computation.12 | async-start | bytes 262144 | tf_op jit(solution)/shard_map/all_to_all | solution.py:131
  173.4 1.0 reduce.4
  174.6 12.9 %all-to-all-done.12 = f32[128,1,256]{2,1,0:T(1,128)S(1)} async-done(((f32[128,1,256]{2,1,0:T(1,128)}), f32[128,1,256]{2,1,0:T(1,128)S(1)}, u32[]{:S(2)}, u32[]{:S(2)}) %all-to-all-start.12) | async-done | bytes 131104 | tf_op jit(solution)/shard_map/all_to_all | solution.py:131
  190.6 17.4 %all_to_all.90 = f32[128,1,128]{2,1,0:T(1,128)S(1)} all-to-all(f32[128,1,128]{2,1,0:T(1,128)S(1)} %reshape.348), channel_id=1, replica_groups=mesh['ctx'=128,'ch'=2] {'ctx'}, dimensions={0} | all-to-all | bytes 131072 | tf_op jit(solution)/shard_map/all_to_all | solution.py:135
  210.7 17.6 %all_to_all.91 = f32[128,1,128]{2,1,0:T(1,128)S(1)} all-to-all(f32[128,1,128]{2,1,0:T(1,128)S(1)} %reshape.326), channel_id=1, replica_groups=mesh['ctx'=128,'ch'=2] {'ctx'}, dimensions={0} | all-to-all | bytes 131072 | tf_op jit(solution)/shard_map/all_to_all | solution.py:98
  232.0 5.8 %all-to-all-start.2 = ((f32[128,1,256]{2,1,0:T(1,128)}), f32[128,1,256]{2,1,0:T(1,128)S(1)}, u32[]{:S(2)}, u32[]{:S(2)}) async-start(f32[128,1,256]{2,1,0:T(1,128)} %reshape.330), calls=%async_computation.2 | async-start | bytes 262144 | tf_op jit(solution)/shard_map/all_to_all | solution.py:110
  238.8 13.0 %all-to-all-done.2 = f32[128,1,256]{2,1,0:T(1,128)S(1)} async-done(((f32[128,1,256]{2,1,0:T(1,128)}), f32[128,1,256]{2,1,0:T(1,128)S(1)}, u32[]{:S(2)}, u32[]{:S(2)}) %all-to-all-start.2) | async-done | bytes 131104 | tf_op jit(solution)/shard_map/all_to_all | solution.py:110
  251.8 6.1 %all-to-all-start.1 = ((f32[128,1,256]{2,1,0:T(1,128)}), f32[128,1,256]{2,1,0:T(1,128)S(1)}, u32[]{:S(2)}, u32[]{:S(2)}) async-start(f32[128,1,256]{2,1,0:T(1,128)} %reshape.328), calls=%async_computation.1 | async-start | bytes 262144 | tf_op jit(solution)/shard_map/all_to_all | solution.py:109
  257.9 1.0 reduce.7
  259.2 1.3 convolution_bitcast_fusion.6
  260.5 11.3 %all-to-all-done.1 = f32[128,1,256]{2,1,0:T(1,128)S(1)} async-done(((f32[128,1,256]{2,1,0:T(1,128)}), f32[128,1,256]{2,1,0:T(1,128)S(1)}, u32[]{:S(2)}, u32[]{:S(2)}) %all-to-all-start.1) | async-done | bytes 131104 | tf_op jit(solution)/shard_map/all_to_all | solution.py:109
  273.1 1.3 convolution_bitcast_fusion.4
  274.4 1.3 fusion
  275.7 1.4 subtract_reduce_fusion
  277.1 3.8 all-reduce
  280.9 1.3 fusion.17
  282.2 1.3 fusion.21
  283.5 1.4 convolution_subtract_fusion.4
  284.9 1.4 multiply_add_fusion.8
  287.1 6.8 %all-to-all-start.15 = ((f32[1,2,256]{1,0,2:T(1,128)}), f32[1,2,256]{1,0,2:T(1,128)S(1)}, u32[]{:S(2)}, u32[]{:S(2)}) async-start(f32[1,2,256]{1,0,2:T(1,128)} %bitcast.58), calls=%async_computation.15 | async-start | bytes 262144 | tf_op jit(solution)/shard_map/all_to_all | solution.py:131
  293.9 1.7 fusion.32
  295.6 1.7 convolution_add_fusion.1
  297.3 1.7 fusion.27
  299.8 8.1 %all-to-all-done.15 = f32[1,2,256]{1,0,2:T(1,128)S(1)} async-done(((f32[1,2,256]{1,0,2:T(1,128)}), f32[1,2,256]{1,0,2:T(1,128)S(1)}, u32[]{:S(2)}, u32[]{:S(2)}) %all-to-all-start.15) | async-done | bytes 2080 | tf_op jit(solution)/shard_map/all_to_all | solution.py:131
  307.9 5.9 %all-to-all-start.16 = ((f32[1,2,256]{1,0,2:T(1,128)}), f32[1,2,256]{1,0,2:T(1,128)S(1)}, u32[]{:S(2)}, u32[]{:S(2)}) async-start(f32[1,2,256]{1,0,2:T(1,128)} %bitcast.60), calls=%async_computation.16 | async-start | bytes 262144 | tf_op jit(solution)/shard_map/all_to_all | solution.py:132
  314.6 13.2 %all-to-all-done.16 = f32[1,2,256]{1,0,2:T(1,128)S(1)} async-done(((f32[1,2,256]{1,0,2:T(1,128)}), f32[1,2,256]{1,0,2:T(1,128)S(1)}, u32[]{:S(2)}, u32[]{:S(2)}) %all-to-all-start.16) | async-done | bytes 2080 | tf_op jit(solution)/shard_map/all_to_all | solution.py:132
  329.2 5.5 %all-to-all-start.17 = ((f32[1,2,128]{1,0,2:T(1,128)}), f32[1,2,128]{1,0,2:T(1,128)S(1)}, u32[]{:S(2)}, u32[]{:S(2)}) async-start(f32[1,2,128]{1,0,2:T(1,128)} %copy.206), calls=%async_computation.17 | async-start | bytes 131072 | tf_op jit(solution)/shard_map/all_to_all | solution.py:135
  334.8 1.7 add_bitcast_fusion.1
  337.8 9.4 %all-to-all-done.17 = f32[1,2,128]{1,0,2:T(1,128)S(1)} async-done(((f32[1,2,128]{1,0,2:T(1,128)}), f32[1,2,128]{1,0,2:T(1,128)S(1)}, u32[]{:S(2)}, u32[]{:S(2)}) %all-to-all-start.17) | async-done | bytes 1056 | tf_op jit(solution)/shard_map/all_to_all | solution.py:135
  347.2 6.1 %all-to-all-start.7 = ((f32[128,1,256]{2,1,0:T(1,128)}), f32[128,1,256]{2,1,0:T(1,128)S(1)}, u32[]{:S(2)}, u32[]{:S(2)}) async-start(f32[128,1,256]{2,1,0:T(1,128)} %reshape.334), calls=%async_computation.7 | async-start | bytes 262144 | tf_op jit(solution)/shard_map/all_to_all | solution.py:132
  354.6 12.6 %all-to-all-done.7 = f32[128,1,256]{2,1,0:T(1,128)S(1)} async-done(((f32[128,1,256]{2,1,0:T(1,128)}), f32[128,1,256]{2,1,0:T(1,128)S(1)}, u32[]{:S(2)}, u32[]{:S(2)}) %all-to-all-start.7) | async-done | bytes 131104 | tf_op jit(solution)/shard_map/all_to_all | solution.py:132
  367.3 5.5 %all-to-all-start.6 = ((f32[128,1,256]{2,1,0:T(1,128)}), f32[128,1,256]{2,1,0:T(1,128)S(1)}, u32[]{:S(2)}, u32[]{:S(2)}) async-start(f32[128,1,256]{2,1,0:T(1,128)} %reshape.332), calls=%async_computation.6 | async-start | bytes 262144 | tf_op jit(solution)/shard_map/all_to_all | solution.py:131
  372.9 1.0 reduce.10
  374.1 12.8 %all-to-all-done.6 = f32[128,1,256]{2,1,0:T(1,128)S(1)} async-done(((f32[128,1,256]{2,1,0:T(1,128)}), f32[128,1,256]{2,1,0:T(1,128)S(1)}, u32[]{:S(2)}, u32[]{:S(2)}) %all-to-all-start.6) | async-done | bytes 131104 | tf_op jit(solution)/shard_map/all_to_all | solution.py:131
  390.7 5.5 %all-to-all-start.8 = ((f32[128,1,128]{2,1,0:T(1,128)}), f32[128,1,128]{2,1,0:T(1,128)S(1)}, u32[]{:S(2)}, u32[]{:S(2)}) async-start(f32[128,1,128]{2,1,0:T(1,128)} %reshape.336), calls=%async_computation.8 | async-start | bytes 131072 | tf_op jit(solution)/shard_map/all_to_all | solution.py:135
  396.7 11.9 %all-to-all-done.8 = f32[128,1,128]{2,1,0:T(1,128)S(1)} async-done(((f32[128,1,128]{2,1,0:T(1,128)}), f32[128,1,128]{2,1,0:T(1,128)S(1)}, u32[]{:S(2)}, u32[]{:S(2)}) %all-to-all-start.8) | async-done | bytes 65568 | tf_op jit(solution)/shard_map/all_to_all | solution.py:135
  (101 shorter events, 40.3 us)
Async XLA Ops:
  0.6 0.7 copy-start.4
  2.0 16.6 %copy-start = (bf16[64,256]{1,0:T(8,128)(2,1)S(1)}, bf16[64,256]{1,0:T(8,128)(2,1)}, u32[]{:S(2)}) copy-start(bf16[64,256]{1,0:T(8,128)(2,1)} %param.9) | copy-start | bytes 98308
  2.0 16.6 %copy-start.1 = (bf16[64,256]{1,0:T(8,128)(2,1)S(1)}, bf16[64,256]{1,0:T(8,128)(2,1)}, u32[]{:S(2)}) copy-start(bf16[64,256]{1,0:T(8,128)(2,1)} %param.5) | copy-start | bytes 98308
  2.0 28.9 %all-to-all-start.3 = ((f32[1,2,128]{1,0,2:T(1,128)}), f32[1,2,128]{1,0,2:T(1,128)S(1)}, u32[]{:S(2)}, u32[]{:S(2)}) async-start(f32[1,2,128]{1,0,2:T(1,128)} %copy.164), calls=%async_computation.3 | async-start | bytes 131072 | tf_op jit(solution)/shard_map/all_to_all | solution.py:98
  33.1 19.9 %all-to-all-start.5 = ((f32[1,2,256]{1,0,2:T(1,128)}), f32[1,2,256]{1,0,2:T(1,128)S(1)}, u32[]{:S(2)}, u32[]{:S(2)}) async-start(f32[1,2,256]{1,0,2:T(1,128)} %copy.168), calls=%async_computation.5 | async-start | bytes 262144 | tf_op jit(solution)/shard_map/all_to_all | solution.py:110
  52.9 19.6 %all-to-all-start.4 = ((f32[1,2,256]{1,0,2:T(1,128)}), f32[1,2,256]{1,0,2:T(1,128)S(1)}, u32[]{:S(2)}, u32[]{:S(2)}) async-start(f32[1,2,256]{1,0,2:T(1,128)} %copy.165), calls=%async_computation.4 | async-start | bytes 262144 | tf_op jit(solution)/shard_map/all_to_all | solution.py:109
  72.5 18.3 %all-to-all-start.9 = ((f32[128,1,128]{2,1,0:T(1,128)}), f32[128,1,128]{2,1,0:T(1,128)S(1)}, u32[]{:S(2)}, u32[]{:S(2)}) async-start(f32[128,1,128]{2,1,0:T(1,128)} %reshape.338), calls=%async_computation.9 | async-start | bytes 131072 | tf_op jit(solution)/shard_map/all_to_all | solution.py:98
  94.9 19.8 %all-to-all-start.11 = ((f32[128,1,256]{2,1,0:T(1,128)}), f32[128,1,256]{2,1,0:T(1,128)S(1)}, u32[]{:S(2)}, u32[]{:S(2)}) async-start(f32[128,1,256]{2,1,0:T(1,128)} %reshape.342), calls=%async_computation.11 | async-start | bytes 262144 | tf_op jit(solution)/shard_map/all_to_all | solution.py:110
  114.7 20.0 %all-to-all-start.10 = ((f32[128,1,256]{2,1,0:T(1,128)}), f32[128,1,256]{2,1,0:T(1,128)S(1)}, u32[]{:S(2)}, u32[]{:S(2)}) async-start(f32[128,1,256]{2,1,0:T(1,128)} %reshape.340), calls=%async_computation.10 | async-start | bytes 262144 | tf_op jit(solution)/shard_map/all_to_all | solution.py:109
  148.2 19.8 %all-to-all-start.13 = ((f32[128,1,256]{2,1,0:T(1,128)}), f32[128,1,256]{2,1,0:T(1,128)S(1)}, u32[]{:S(2)}, u32[]{:S(2)}) async-start(f32[128,1,256]{2,1,0:T(1,128)} %reshape.346), calls=%async_computation.13 | async-start | bytes 262144 | tf_op jit(solution)/shard_map/all_to_all | solution.py:132
  167.9 19.6 %all-to-all-start.12 = ((f32[128,1,256]{2,1,0:T(1,128)}), f32[128,1,256]{2,1,0:T(1,128)S(1)}, u32[]{:S(2)}, u32[]{:S(2)}) async-start(f32[128,1,256]{2,1,0:T(1,128)} %reshape.344), calls=%async_computation.12 | async-start | bytes 262144 | tf_op jit(solution)/shard_map/all_to_all | solution.py:131
  209.0 0.8 copy-start.2
  209.0 0.8 copy-start.3
  232.0 19.8 %all-to-all-start.2 = ((f32[128,1,256]{2,1,0:T(1,128)}), f32[128,1,256]{2,1,0:T(1,128)S(1)}, u32[]{:S(2)}, u32[]{:S(2)}) async-start(f32[128,1,256]{2,1,0:T(1,128)} %reshape.330), calls=%async_computation.2 | async-start | bytes 262144 | tf_op jit(solution)/shard_map/all_to_all | solution.py:110
  251.8 20.0 %all-to-all-start.1 = ((f32[128,1,256]{2,1,0:T(1,128)}), f32[128,1,256]{2,1,0:T(1,128)S(1)}, u32[]{:S(2)}, u32[]{:S(2)}) async-start(f32[128,1,256]{2,1,0:T(1,128)} %reshape.328), calls=%async_computation.1 | async-start | bytes 262144 | tf_op jit(solution)/shard_map/all_to_all | solution.py:109
  287.1 20.9 %all-to-all-start.15 = ((f32[1,2,256]{1,0,2:T(1,128)}), f32[1,2,256]{1,0,2:T(1,128)S(1)}, u32[]{:S(2)}, u32[]{:S(2)}) async-start(f32[1,2,256]{1,0,2:T(1,128)} %bitcast.58), calls=%async_computation.15 | async-start | bytes 262144 | tf_op jit(solution)/shard_map/all_to_all | solution.py:131
  307.9 19.9 %all-to-all-start.16 = ((f32[1,2,256]{1,0,2:T(1,128)}), f32[1,2,256]{1,0,2:T(1,128)S(1)}, u32[]{:S(2)}, u32[]{:S(2)}) async-start(f32[1,2,256]{1,0,2:T(1,128)} %bitcast.60), calls=%async_computation.16 | async-start | bytes 262144 | tf_op jit(solution)/shard_map/all_to_all | solution.py:132
  329.2 18.0 %all-to-all-start.17 = ((f32[1,2,128]{1,0,2:T(1,128)}), f32[1,2,128]{1,0,2:T(1,128)S(1)}, u32[]{:S(2)}, u32[]{:S(2)}) async-start(f32[1,2,128]{1,0,2:T(1,128)} %copy.206), calls=%async_computation.17 | async-start | bytes 131072 | tf_op jit(solution)/shard_map/all_to_all | solution.py:135
  347.2 20.0 %all-to-all-start.7 = ((f32[128,1,256]{2,1,0:T(1,128)}), f32[128,1,256]{2,1,0:T(1,128)S(1)}, u32[]{:S(2)}, u32[]{:S(2)}) async-start(f32[128,1,256]{2,1,0:T(1,128)} %reshape.334), calls=%async_computation.7 | async-start | bytes 262144 | tf_op jit(solution)/shard_map/all_to_all | solution.py:132
  367.3 19.6 %all-to-all-start.6 = ((f32[128,1,256]{2,1,0:T(1,128)}), f32[128,1,256]{2,1,0:T(1,128)S(1)}, u32[]{:S(2)}, u32[]{:S(2)}) async-start(f32[128,1,256]{2,1,0:T(1,128)} %reshape.332), calls=%async_computation.6 | async-start | bytes 262144 | tf_op jit(solution)/shard_map/all_to_all | solution.py:131
  390.7 18.0 %all-to-all-start.8 = ((f32[128,1,128]{2,1,0:T(1,128)}), f32[128,1,128]{2,1,0:T(1,128)S(1)}, u32[]{:S(2)}, u32[]{:S(2)}) async-start(f32[128,1,128]{2,1,0:T(1,128)} %reshape.336), calls=%async_computation.8 | async-start | bytes 131072 | tf_op jit(solution)/shard_map/all_to_all | solution.py:135
where the time goes:
time: 419 us; the launch traced here: 411 us
  waiting for transfers between devices  186 us (44%)
  starting transfers between devices  104 us (25%)
  matrix products  44 us (11%)
  blocking collectives  38.8 us (9%)
  local copies, waits for them, and re-layouts  22.9 us (5%)
  other arithmetic  12.9 us (3%)
    dot_general x36, matrix products, contract(): jnp.einsum(pattern, former, latter, precision=lax.Precision.HIGHEST, pref...  44 us
    all_to_all x3, waiting for transfers between devices, restore(): lax.all_to_all(turned_imag, 'ctx', split_axis=2, concat_axis=2, tiled=True)  38.6 us
    all_to_all x3, waiting for transfers between devices, transform(): lax.all_to_all(front_imag, 'ctx', split_axis=2, concat_axis=2, tiled=True)  36.5 us
    all_to_all x3, waiting for transfers between devices, restore(): lax.all_to_all(turned_real, 'ctx', split_axis=2, concat_axis=2, tiled=True)  33.8 us
    all_to_all x3, waiting for transfers between devices, transform(): lax.all_to_all(front_real, 'ctx', split_axis=2, concat_axis=2, tiled=True)  33.5 us
    all_to_all x2, waiting for transfers between devices, transform(): lax.all_to_all(signal.reshape(signal.shape[0], stripes, groups), 'ctx', s...  22.5 us
    all_to_all x2, starting transfers between devices, transform(): lax.all_to_all(signal.reshape(signal.shape[0], stripes, groups), 'ctx', s...  22.4 us
    all_to_all x2, waiting for transfers between devices, restore(): lax.all_to_all(values, 'ctx', split_axis=2, concat_axis=2, tiled=True)  21.3 us
  transfers between devices with their start and end apart: 16, of which 16 were waited for; matrix products, arithmetic and copies ran while one was open for 8% of the time, Pallas kernels for 0%

commit v1 on v0

v1 whole, which is shorter than its diff:
```python
import math

import jax
import jax.numpy as jnp
import numpy as np
from jax import lax
from jax.experimental import pallas as pl
from jax.experimental.pallas import tpu as pltpu
from jax.sharding import PartitionSpec as P

SHIFT = 0.25


def halves(values):
    high = values.astype(jnp.bfloat16)
    low = (values - np.asarray(high).astype(np.float64)).astype(jnp.bfloat16)
    return np.asarray(high), np.asarray(low)


def tables(blocks, width):
    length = blocks * width
    rows = np.arange(blocks) + SHIFT
    block_angle = 2.0 * math.pi * np.outer(rows, np.arange(blocks)) / blocks
    forward = np.concatenate([np.cos(block_angle), -np.sin(block_angle)], axis=0)
    backward = np.concatenate([np.cos(block_angle), -np.sin(block_angle)], axis=0).T / length
    own = [np.arange(parity, blocks, 2) for parity in (0, 1)]
    ahead = np.stack([np.concatenate([forward[:, own[e]], forward[:, own[1 - e]]], 1) for e in (0, 1)])
    back = np.stack([backward[own[e], :] for e in (0, 1)])
    ahead_high, ahead_low = halves(ahead)
    back_high, back_low = halves(back)
    ahead_table = np.concatenate([ahead_high, ahead_high, ahead_low], axis=2)
    back_table = np.concatenate([back_high, back_high, back_low], axis=2)
    twist_angle = 2.0 * math.pi * np.outer(rows, np.arange(width)) / length
    twist = np.stack([np.cos(twist_angle), np.sin(twist_angle)]).astype(np.float32)
    inner_angle = 2.0 * math.pi * (np.outer(np.arange(width), np.arange(width)) % width) / width
    inner_high, inner_low = halves(np.concatenate([np.cos(inner_angle), np.sin(inner_angle)], axis=1))
    return ahead_table, back_table, twist, np.stack([inner_high, inner_low])


def split(values):
    high = values.astype(jnp.bfloat16)
    return high, (values - high.astype(jnp.float32)).astype(jnp.bfloat16)


def dot(left, right):
    return jnp.dot(left, right, preferred_element_type=jnp.float32)


def inner_dot(values, inner_ref):
    high, low = split(values)
    return dot(high, inner_ref[0]) + dot(low, inner_ref[0]) + dot(high, inner_ref[1])


def pack_body(query_ref, key_ref, value_ref, grad_ref, taps_ref, out_ref):
    width = query_ref.shape[1]
    out_ref[:, 0, :width] = key_ref[...].astype(jnp.float32) * value_ref[...].astype(jnp.float32)
    out_ref[:, 0, width : 2 * width] = grad_ref[...].astype(jnp.float32) * query_ref[...].astype(jnp.float32)
    out_ref[:, 0, 2 * width :] = jnp.broadcast_to(taps_ref[...], query_ref.shape)


def middle_body(scale, parity_ref, own_ref, other_ref, ahead_ref, back_ref, twist_ref, inner_ref, out_ref):
    parity = parity_ref[0]
    width = twist_ref.shape[2]
    rows = twist_ref.shape[1]
    signal = jnp.concatenate([own_ref[:, 0, :], other_ref[:, 0, :]], axis=0)
    high, low = split(signal)
    front = dot(ahead_ref[parity], jnp.concatenate([high, low, high], axis=0))
    cosine, sine = twist_ref[0], twist_ref[1]
    turned = []
    for index in range(3):
        real = front[:rows, index * width : (index + 1) * width]
        imag = front[rows:, index * width : (index + 1) * width]
        turned += [real * cosine + imag * sine, imag * cosine - real * sine]
    product = inner_dot(jnp.concatenate(turned, axis=0), inner_ref)
    spectra = []
    for index in range(3):
        real = product[2 * index * rows : (2 * index + 1) * rows]
        imag = product[(2 * index + 1) * rows : (2 * index + 2) * rows]
        spectra.append((real[:, :width] + imag[:, width:], imag[:, :width] - real[:, width:]))
    (gated_real, gated_imag), (grad_real, grad_imag), (taps_real, taps_imag) = spectra
    mixed = [
        gated_real * taps_real - gated_imag * taps_imag,
        gated_real * taps_imag + gated_imag * taps_real,
        grad_real * taps_real + grad_imag * taps_imag,
        grad_imag * taps_real - grad_real * taps_imag,
        (grad_real * gated_real + grad_imag * gated_imag) * scale,
        (grad_imag * gated_real - grad_real * gated_imag) * scale,
    ]
    product = inner_dot(jnp.concatenate(mixed, axis=0), inner_ref)
    waves = []
    for index in range(3):
        real = product[2 * index * rows : (2 * index + 1) * rows]
        imag = product[(2 * index + 1) * rows : (2 * index + 2) * rows]
        wave_real = real[:, :width] - imag[:, width:]
        wave_imag = imag[:, :width] + real[:, width:]
        waves.append(
            jnp.concatenate([wave_real * cosine - wave_imag * sine, wave_real * sine + wave_imag * cosine], axis=0)
        )
    high, low = split(jnp.concatenate(waves, axis=1))
    out_ref[:, 0, :] = dot(back_ref[parity], jnp.concatenate([high, low, high], axis=0))


def finish_body(moved_ref, key_ref, value_ref, grad_ref, query_out, key_out, value_out, filter_out):
    width = key_ref.shape[1]
    conv = moved_ref[:, 0, :width]
    back = moved_ref[:, 0, width : 2 * width]
    query_out[...] = (grad_ref[...].astype(jnp.float32) * conv).astype(jnp.bfloat16)
    key_out[...] = (back * value_ref[...].astype(jnp.float32)).astype(jnp.bfloat16)
    value_out[...] = (back * key_ref[...].astype(jnp.float32)).astype(jnp.bfloat16)
    filter_out[...] = jnp.sum(moved_ref[:, 0, 2 * width :], axis=0, keepdims=True)


def shards(query_proj, key_proj, value_proj, filter_taps, out_grad):
    devices = lax.axis_size("ctx")
    channels, width = query_proj.shape
    chips = devices // 2
    parity = (lax.axis_index("ctx") % 2).astype(jnp.int32).reshape(1)
    same_core = [[2 * chip + core for chip in range(chips)] for core in (0, 1)]
    other_core = [(device, device ^ 1) for device in range(devices)]
    total = channels * lax.axis_size("ch") * devices * width
    message = jax.ShapeDtypeStruct((chips, 1, 3 * width), jnp.float32)

    def exchange(array):
        return lax.all_to_all(array, "ctx", 0, 0, axis_index_groups=same_core, tiled=True)

    packed = pl.pallas_call(pack_body, out_shape=message)(
        query_proj, key_proj, value_proj, out_grad, filter_taps.reshape(1, width)
    )
    own = exchange(packed)
    other = lax.ppermute(own, "ctx", other_core)
    in_smem = pl.BlockSpec(memory_space=pltpu.SMEM)
    in_vmem = pl.BlockSpec(memory_space=pltpu.VMEM)
    constants = [jnp.asarray(table) for table in tables(devices, width)]

    def middle(*refs):
        middle_body(1.0 / math.sqrt(total), *refs)

    restored = pl.pallas_call(
        middle,
        out_shape=message,
        in_specs=[in_smem] + [in_vmem] * 6,
        out_specs=in_vmem,
        compiler_params=pltpu.CompilerParams(vmem_limit_bytes=40 * 1024 * 1024),
    )(parity, own, other, *constants)
    moved = exchange(restored)
    narrow = jax.ShapeDtypeStruct((channels, width), jnp.bfloat16)
    query_grad, key_grad, value_grad, partial = pl.pallas_call(
        finish_body,
        out_shape=(narrow, narrow, narrow, jax.ShapeDtypeStruct((1, width), jnp.float32)),
    )(moved, key_proj, value_proj, out_grad)
    partial = partial.reshape(width)
    filter_grad = partial + lax.ppermute(partial, "ch", [(0, 1), (1, 0)])
    return (query_grad, key_grad, value_grad, filter_grad)


def solution(mesh):
    placed = (P("ch", "ctx"), P("ch", "ctx"), P("ch", "ctx"), P("ctx"), P("ch", "ctx"))
    return jax.shard_map(
        shards,
        mesh=mesh,
        in_specs=placed,
        out_specs=(P("ch", "ctx"), P("ch", "ctx"), P("ch", "ctx"), P("ctx")),
        check_vma=False,
    )
```

time: 419 us -> 62 us (0.15)
  the two profiles are of different devices: /device:TPU:1 before, /device:TPU:32 now
where the time goes in v1:
time: 62 us; the launch traced here: 61.7 us
  blocking collectives  46.3 us (75%)
  Pallas kernels  6.52 us (11%)
  waiting for transfers between devices  4.41 us (7%)
  local copies, waits for them, and re-layouts  2.64 us (4%)
  between operations  0.66 us (1%)
    all_to_all x2, blocking collectives, exchange(): lax.all_to_all(array, 'ctx', 0, 0, axis_index_groups=same_core, tiled=True)  46.3 us
    pallas_call x1, Pallas kernels, shards(): pl.pallas_call(middle, out_shape=message, in_specs=[in_smem] + [in_vmem]...  3.29 us
    ppermute x1, waiting for transfers between devices, shards(): filter_grad = partial + lax.ppermute(partial, 'ch', [(0, 1), (1, 0)])  2.97 us
    unnamed x10, local copies, waits for them, and re-layouts  2.64 us
    pallas_call x1, Pallas kernels, shards(): pl.pallas_call(finish_body, out_shape=(narrow, narrow, narrow, jax.ShapeD...  1.63 us
    pallas_call x1, Pallas kernels, shards(): pl.pallas_call(pack_body, out_shape=message)  1.6 us
    ppermute x1, waiting for transfers between devices, shards(): other = lax.ppermute(own, 'ctx', other_core)  1.44 us
  transfers between devices with their start and end apart: 2, of which 2 were waited for; matrix products, arithmetic and copies ran while one was open for 0% of the time, Pallas kernels for 0%

profile of v1, /device:TPU:32, one launch (start us, length us, event | category | flops | bytes accessed | tf_op | source)
XLA Modules:
  0.0 61.7 jit_solution(6641556511057689444)
XLA Ops:
  0.6 0.0 copy-start
  0.6 1.6 %shard_map.120 = f32[64,1,768]{2,1,0:T(1,128)} custom-call(bf16[64,256]{1,0:T(8,128)(2,1)} %query_ref.1, bf16[64,256]{1,0:T(8,128)(2,1)} %key_ref.3, bf16[64,256]{1,0:T(8,128)(2,1)} %value_ref.3, bf16[64,256]{1,0:T(8,128)(2,1)} %grad_ref.3, f32[1,256]{1,0:T(1,128)} %bitcast.3), custom_call_target="tpu_custom_call" | custom-call | tf_op jit(solution)/shard_map/pallas_call | solution.py:126
  2.2 0.0 copy-start.3
  2.2 27.7 %all_to_all.10.refs_1_ = f32[64,1,768]{2,1,0:T(1,128)S(1)} all-to-all(f32[64,1,768]{2,1,0:T(1,128)} %shard_map.120), channel_id=1, replica_groups={{0,4,8,12,16,20,24,28,32,36,40,44,48,52,56,60,64,68,72,76,80,84,88,92,9..., dimensions={0} | all-to-all | bytes 393216 | tf_op jit(solution)/shard_map/all_to_all | solution.py:124
  29.9 0.0 collective-permute-start
  29.9 1.4 %collective-permute-done.refs_2_ = f32[64,1,768]{2,1,0:T(1,128)S(1)} collective-permute-done((f32[64,1,768]{2,1,0:T(1,128)S(1)}, f32[64,1,768]{2,1,0:T(1,128)S(1)}, u32[]{:S(2)}, u32[]{:S(2)}) %collective-permute-start) | collective-permute-done | bytes 196640 | tf_op jit(solution)/shard_map/ppermute | solution.py:130
  31.4 0.0 copy-done
  31.4 0.0 copy-done.3
  31.4 0.0 copy-start.1
  31.4 1.0 %copy-done.1 = bf16[2,256,384]{2,1,0:T(8,128)(2,1)S(1)} copy-done((bf16[2,256,384]{2,1,0:T(8,128)(2,1)S(1)}, bf16[2,256,384]{2,1,0:T(8,128)(2,1)}, u32[]{:S(2)}) %copy-start.1) | copy-done | bytes 393240
  32.4 0.0 copy-start.2
  32.4 0.9 %copy-done.2 = f32[2,128,256]{2,1,0:T(8,128)S(1)} copy-done((f32[2,128,256]{2,1,0:T(8,128)S(1)}, f32[2,128,256]{2,1,0:T(8,128)}, u32[]{:S(2)}) %copy-start.2) | copy-done | bytes 262168
  33.3 3.3 %shard_map.121 = f32[64,1,768]{2,1,0:T(1,128)S(1)} custom-call(s32[1]{0:T(128)} %bitcast.refs_0_, f32[64,1,768]{2,1,0:T(1,128)S(1)} %all_to_all.10.refs_1_, f32[64,1,768]{2,1,0:T(1,128)S(1)} %collective-permute-done.refs_2_, bf16[2,256,384]{2,1,0:T(8,128)(2,1)S(1)} %copy-done.1, bf16[2,64,768]{2,1,0:T(8,128)(2,1)S(1)} %copy-done.3, ...), custom_call_target="tpu_custom_call" | custom-call | tf_op jit(solution)/shard_map/pallas_call | solution.py:138
  36.6 18.6 %all_to_all.11.moved_ref = f32[64,1,768]{2,1,0:T(1,128)} all-to-all(f32[64,1,768]{2,1,0:T(1,128)S(1)} %shard_map.121), channel_id=1, replica_groups={{0,4,8,12,16,20,24,28,32,36,40,44,48,52,56,60,64,68,72,76,80,84,88,92,9..., dimensions={0} | all-to-all | bytes 393216 | tf_op jit(solution)/shard_map/all_to_all | solution.py:124
  55.3 1.6 %shard_map.122 = (bf16[64,256]{1,0:T(8,128)(2,1)}, bf16[64,256]{1,0:T(8,128)(2,1)}, bf16[64,256]{1,0:T(8,128)(2,1)}, f32[1,256]{1,0:T(1,128)}) custom-call(f32[64,1,768]{2,1,0:T(1,128)} %all_to_all.11.moved_ref, bf16[64,256]{1,0:T(8,128)(2,1)} %key_ref.3, bf16[64,256]{1,0:T(8,128)(2,1)} %value_ref.3, bf16[64,256]{1,0:T(8,128)(2,1)} %grad_ref.3), custom_call_target="tpu_custom_call" | custom-call | tf_op jit(solution)/shard_map/pallas_call | solution.py:147
  56.9 0.0 copy-start.4
  56.9 0.7 %copy-done.4 = f32[1,256]{1,0:T(1,128)S(1)} copy-done((f32[1,256]{1,0:T(1,128)S(1)}, f32[1,256]{1,0:T(1,128)}, u32[]{:S(2)}) %copy-start.4) | copy-done | bytes 1048
  57.6 0.6 collective-permute-start.1
  58.2 3.0 %collective-permute-done.1 = f32[256]{0:T(256)S(1)} collective-permute-done((f32[256]{0:T(256)S(1)}, f32[256]{0:T(256)S(1)}, u32[]{:S(2)}, u32[]{:S(2)}) %collective-permute-start.1) | collective-permute-done | bytes 1056 | tf_op jit(solution)/shard_map/ppermute | solution.py:152
  61.1 0.6 add.8
Async XLA Ops:
  0.6 30.7 %copy-start = (bf16[2,256,512]{2,1,0:T(8,128)(2,1)S(1)}, bf16[2,256,512]{2,1,0:T(8,128)(2,1)}, u32[]{:S(2)}) copy-start(bf16[2,256,512]{2,1,0:T(8,128)(2,1)} %constant.30.clone.refs_6_) | copy-start | bytes 1572868
  2.2 29.1 %copy-start.3 = (bf16[2,64,768]{2,1,0:T(8,128)(2,1)S(1)}, bf16[2,64,768]{2,1,0:T(8,128)(2,1)}, u32[]{:S(2)}) copy-start(bf16[2,64,768]{2,1,0:T(8,128)(2,1)} %constant.28.clone.refs_4_) | copy-start | bytes 589828
  29.9 1.4 %collective-permute-start = (f32[64,1,768]{2,1,0:T(1,128)S(1)}, f32[64,1,768]{2,1,0:T(1,128)S(1)}, u32[]{:S(2)}, u32[]{:S(2)}) collective-permute-start(f32[64,1,768]{2,1,0:T(1,128)S(1)} %all_to_all.10.refs_1_), channel_id=1, source_target_pairs={{0,2},{2,0},{4,6},{6,4},{8,10},{10,8},{12,14},{14,12},{16,18},{18,... | collective-permute-start | bytes 589832 | tf_op jit(solution)/shard_map/ppermute | solution.py:130
  31.4 1.0 %copy-start.1 = (bf16[2,256,384]{2,1,0:T(8,128)(2,1)S(1)}, bf16[2,256,384]{2,1,0:T(8,128)(2,1)}, u32[]{:S(2)}) copy-start(bf16[2,256,384]{2,1,0:T(8,128)(2,1)} %constant.27.clone.refs_3_) | copy-start | bytes 1179652
  32.4 0.9 %copy-start.2 = (f32[2,128,256]{2,1,0:T(8,128)S(1)}, f32[2,128,256]{2,1,0:T(8,128)}, u32[]{:S(2)}) copy-start(f32[2,128,256]{2,1,0:T(8,128)} %constant.29.clone.refs_5_) | copy-start | bytes 786436
  56.9 0.7 %copy-start.4 = (f32[1,256]{1,0:T(1,128)S(1)}, f32[1,256]{1,0:T(1,128)}, u32[]{:S(2)}) copy-start(f32[1,256]{1,0:T(1,128)} %get-tuple-element.11) | copy-start | bytes 3076
  57.6 3.6 %collective-permute-start.1 = (f32[256]{0:T(256)S(1)}, f32[256]{0:T(256)S(1)}, u32[]{:S(2)}, u32[]{:S(2)}) collective-permute-start(f32[256]{0:T(256)S(1)} %bitcast.4), channel_id=1, source_target_pairs={{0,1},{1,0},{2,3},{3,2},{4,5},{5,4},{6,7},{7,6},{8,9},{9,8},{10,11... | collective-permute-start | bytes 3080 | tf_op jit(solution)/shard_map/ppermute | solution.py:152

commit v2 on v1

v2 whole, which is shorter than its diff:
```python
import math

import jax
import jax.numpy as jnp
import numpy as np
from jax import lax
from jax.experimental import pallas as pl
from jax.experimental.pallas import tpu as pltpu
from jax.sharding import PartitionSpec as P

SHIFT = 0.25
MIB = 1024 * 1024
AHEAD, BACK, TWIST = 4, 8, 9


def halves(values):
    high = values.astype(jnp.bfloat16)
    low = (values - np.asarray(high).astype(np.float64)).astype(jnp.bfloat16)
    return np.asarray(high), np.asarray(low)


def table_bank(blocks, width):
    length = blocks * width
    half = width // 2
    rows = np.arange(blocks) + SHIFT
    planes = []
    for odd in (0, 1):
        angle = 2.0 * math.pi * (np.outer(np.arange(half), 2 * np.arange(half) + odd) % width) / width
        cosine, sine = np.cos(angle), np.sin(angle)
        planes += halves(np.block([[cosine, -sine], [sine, cosine]]))
    block_angle = 2.0 * math.pi * np.outer(rows, np.arange(blocks)) / blocks
    block_table = np.concatenate([np.cos(block_angle), -np.sin(block_angle)], axis=0)
    own = [np.arange(parity, blocks, 2) for parity in (0, 1)]
    for e in (0, 1):
        high, low = halves(np.concatenate([block_table[:, own[e]], block_table[:, own[1 - e]]], axis=1))
        planes += [np.concatenate([high, high], axis=1), np.concatenate([low, np.zeros_like(low)], axis=1)]
    pieces = [np.concatenate(halves(block_table.T[own[e]] / length), axis=0) for e in (0, 1)]
    planes.append(np.concatenate(pieces, axis=0))
    twist_angle = 2.0 * math.pi * np.outer(rows, np.arange(width)) / length
    planes += [np.concatenate(halves(np.cos(twist_angle)), axis=0), np.concatenate(halves(np.sin(twist_angle)), axis=0)]
    return np.stack(planes)


def split(values):
    high = values.astype(jnp.bfloat16)
    return high, (values - high.astype(jnp.float32)).astype(jnp.bfloat16)


def product(left, right, transposed=False):
    contracted = (((1,), (1 if transposed else 0,)), ((), ()))
    return lax.dot_general(left, right, contracted, preferred_element_type=jnp.float32)


def inner_product(values, bank_ref, odd, transposed):
    count = values.shape[0]
    high, low = split(values)
    wide = product(jnp.concatenate([high, low], axis=0), bank_ref[2 * odd], transposed)
    return wide[:count] + wide[count:] + product(high, bank_ref[2 * odd + 1], transposed)


def pack_body(query_ref, key_ref, value_ref, grad_ref, taps_ref, out_ref):
    width = query_ref.shape[1]
    out_ref[:, 0, :width] = key_ref[...].astype(jnp.float32) * value_ref[...].astype(jnp.float32)
    out_ref[:, 0, width : 2 * width] = grad_ref[...].astype(jnp.float32) * query_ref[...].astype(jnp.float32)
    out_ref[:, 0, 2 * width :] = jnp.broadcast_to(taps_ref[...], query_ref.shape)


def middle_body(scale, parity_ref, own_ref, other_ref, bank_ref, out_ref):
    parity = parity_ref[0]
    width = bank_ref.shape[2]
    half = width // 2
    rows = 2 * own_ref.shape[0]
    high, low = split(jnp.concatenate([own_ref[:, 0, :], other_ref[:, 0, :]], axis=0))
    ahead = bank_ref[pl.ds(AHEAD + 2 * parity, 2)].reshape(2 * width, width)
    front = product(ahead, jnp.concatenate([high, low], axis=0))
    front = front[: 2 * rows] + front[2 * rows :]
    twist = [bank_ref[TWIST + i].astype(jnp.float32) for i in (0, 1)]
    cosine, sine = [table[:rows] + table[rows:] for table in twist]
    even, odd = [], []
    for index in range(3):
        real = front[:rows, index * width : (index + 1) * width]
        imag = front[rows:, index * width : (index + 1) * width]
        real, imag = real * cosine + imag * sine, imag * cosine - real * sine
        even.append(jnp.concatenate([real[:, :half] + real[:, half:], imag[:, :half] + imag[:, half:]], axis=1))
        odd.append(jnp.concatenate([real[:, :half] - real[:, half:], imag[:, :half] - imag[:, half:]], axis=1))
    waves = []
    for bins, stacked in enumerate((even, odd)):
        spectra = inner_product(jnp.concatenate(stacked, axis=0), bank_ref, bins, False)
        gated_real, gated_imag = spectra[:rows, :half], spectra[:rows, half:]
        grad_real, grad_imag = spectra[rows : 2 * rows, :half], spectra[rows : 2 * rows, half:]
        taps_real, taps_imag = spectra[2 * rows :, :half], spectra[2 * rows :, half:]
        conv_real = gated_real * taps_real - gated_imag * taps_imag
        conv_imag = gated_real * taps_imag + gated_imag * taps_real
        back_real = grad_real * taps_real + grad_imag * taps_imag
        back_imag = grad_imag * taps_real - grad_real * taps_imag
        cross_real = (grad_real * gated_real + grad_imag * gated_imag) * scale
        cross_imag = (grad_imag * gated_real - grad_real * gated_imag) * scale
        mixed = jnp.concatenate(
            [
                jnp.concatenate([conv_real, conv_imag], axis=1),
                jnp.concatenate([back_real, back_imag], axis=1),
                jnp.concatenate([cross_real, cross_imag], axis=1),
            ],
            axis=0,
        )
        waves.append(inner_product(mixed, bank_ref, bins, True))
    turned = []
    for index in range(3):
        first = waves[0][index * rows : (index + 1) * rows]
        second = waves[1][index * rows : (index + 1) * rows]
        total, difference = first + second, first - second
        real = jnp.concatenate([total[:, :half], difference[:, :half]], axis=1)
        imag = jnp.concatenate([total[:, half:], difference[:, half:]], axis=1)
        turned.append(jnp.concatenate([real * cosine - imag * sine, real * sine + imag * cosine], axis=0))
    high, low = split(jnp.concatenate(turned, axis=1))
    table = bank_ref[BACK, pl.ds(pl.multiple_of(rows * parity, rows), rows)]
    wide = product(table, high)
    out_ref[:, 0, :] = wide[: rows // 2] + wide[rows // 2 :] + product(table[: rows // 2], low)


def sum_body(moved_ref, out_ref):
    width = out_ref.shape[1]
    out_ref[...] = jnp.sum(moved_ref[:, 0, 2 * width :], axis=0, keepdims=True)


def finish_body(moved_ref, key_ref, value_ref, grad_ref, query_out, key_out, value_out):
    width = key_ref.shape[1]
    conv = moved_ref[:, 0, :width]
    back = moved_ref[:, 0, width : 2 * width]
    query_out[...] = (grad_ref[...].astype(jnp.float32) * conv).astype(jnp.bfloat16)
    key_out[...] = (back * value_ref[...].astype(jnp.float32)).astype(jnp.bfloat16)
    value_out[...] = (back * key_ref[...].astype(jnp.float32)).astype(jnp.bfloat16)


def kernel_call(body, out_shape, limit, operands, in_specs=None):
    placed = {} if in_specs is None else {"in_specs": in_specs}
    return pl.pallas_call(
        body,
        out_shape=out_shape,
        compiler_params=pltpu.CompilerParams(vmem_limit_bytes=limit * MIB),
        **placed,
    )(*operands)


def shards(query_proj, key_proj, value_proj, filter_taps, out_grad):
    devices = lax.axis_size("ctx")
    channels, width = query_proj.shape
    chips = devices // 2
    parity = (lax.axis_index("ctx") % 2).astype(jnp.int32).reshape(1)
    same_core = [[2 * chip + core for chip in range(chips)] for core in (0, 1)]
    other_core = [(device, device ^ 1) for device in range(devices)]
    scale = 1.0 / math.sqrt(channels * lax.axis_size("ch") * devices * width)
    message = jax.ShapeDtypeStruct((chips, 1, 3 * width), jnp.float32)
    narrow = jax.ShapeDtypeStruct((channels, width), jnp.bfloat16)
    bank = jnp.asarray(table_bank(devices, width))

    def exchange(array):
        return lax.all_to_all(array, "ctx", 0, 0, axis_index_groups=same_core, tiled=True)

    def middle(*refs):
        middle_body(scale, *refs)

    taps = filter_taps.reshape(1, width)
    packed = kernel_call(pack_body, message, 4, (query_proj, key_proj, value_proj, out_grad, taps))
    own = exchange(packed)
    other = lax.ppermute(own, "ctx", other_core)
    in_smem = pl.BlockSpec(memory_space=pltpu.SMEM)
    in_vmem = pl.BlockSpec(memory_space=pltpu.VMEM)
    restored = kernel_call(middle, message, 24, (parity, own, other, bank), [in_smem, in_vmem, in_vmem, in_vmem])
    moved = exchange(restored)
    partial = kernel_call(sum_body, jax.ShapeDtypeStruct((1, width), jnp.float32), 4, (moved,)).reshape(width)
    swapped = lax.ppermute(partial, "ch", [(0, 1), (1, 0)])
    query_grad, key_grad, value_grad = kernel_call(
        finish_body, (narrow, narrow, narrow), 4, (moved, key_proj, value_proj, out_grad)
    )
    return (query_grad, key_grad, value_grad, partial + swapped)


def solution(mesh):
    placed = (P("ch", "ctx"), P("ch", "ctx"), P("ch", "ctx"), P("ctx"), P("ch", "ctx"))
    return jax.shard_map(
        shards,
        mesh=mesh,
        in_specs=placed,
        out_specs=(P("ch", "ctx"), P("ch", "ctx"), P("ch", "ctx"), P("ctx")),
        check_vma=False,
    )
```

time: 62 us -> 59.6 us (0.961)
  Pallas kernels: 6.52 us -> 2.62 us
  local copies, waits for them, and re-layouts: 2.64 us -> 5.08 us
  waiting for transfers between devices: 4.41 us -> 3.72 us
    pallas_call x3 -> x4, Pallas kernels: 6.52 us -> 2.62 us  [kernel_call(): pl.pallas_call(body, out_shape=out_shape, compiler_params=pltpu.CompilerP...]
    unnamed x10 -> x18, local copies, waits for them, and re-layouts: 2.64 us -> 5.08 us
    ppermute x1, waiting for transfers between devices: 2.97 us -> 2.29 us  [shards(): swapped = lax.ppermute(partial, 'ch', [(0, 1), (1, 0)])]
  transfers between devices with their start and end apart: 2 -> 2, of which waited for: 2 -> 2; matrix products, arithmetic and copies ran while one was open for 0% -> 0% of each run, Pallas kernels for 0% -> 1%
where the time goes in v2:
time: 59.6 us; the launch traced here: 59.1 us
  blocking collectives  45.7 us (77%)
  local copies, waits for them, and re-layouts  5.08 us (9%)
  waiting for transfers between devices  3.72 us (6%)
  Pallas kernels  2.62 us (4%)
  starting transfers between devices  0.68 us (1%)
  between operations  0.68 us (1%)
    all_to_all x2, blocking collectives, exchange(): lax.all_to_all(array, 'ctx', 0, 0, axis_index_groups=same_core, tiled=True)  45.7 us
    unnamed x18, local copies, waits for them, and re-layouts  5.08 us
    pallas_call x4, Pallas kernels, kernel_call(): pl.pallas_call(body, out_shape=out_shape, compiler_params=pltpu.CompilerP...  2.62 us
    ppermute x1, waiting for transfers between devices, shards(): swapped = lax.ppermute(partial, 'ch', [(0, 1), (1, 0)])  2.29 us
    ppermute x1, waiting for transfers between devices, shards(): other = lax.ppermute(own, 'ctx', other_core)  1.44 us
  transfers between devices with their start and end apart: 2, of which 2 were waited for; matrix products, arithmetic and copies ran while one was open for 0% of the time, Pallas kernels for 1%

profile of v2, /device:TPU:32, one launch (start us, length us, event | category | flops | bytes accessed | tf_op | source)
XLA Modules:
  0.0 59.1 jit_solution(7936140997005752366)
XLA Ops:
  0.6 0.0 copy-start.1
  0.6 0.7 %copy-done.1 = bf16[64,256]{1,0:T(8,128)(2,1)S(1)} copy-done((bf16[64,256]{1,0:T(8,128)(2,1)S(1)}, bf16[64,256]{1,0:T(8,128)(2,1)}, u32[]{:S(2)}) %copy-start.1) | copy-done | bytes 32792
  1.4 0.0 copy-start.3
  1.4 0.8 %copy-done.3 = bf16[64,256]{1,0:T(8,128)(2,1)S(1)} copy-done((bf16[64,256]{1,0:T(8,128)(2,1)S(1)}, bf16[64,256]{1,0:T(8,128)(2,1)}, u32[]{:S(2)}) %copy-start.3) | copy-done | bytes 32792
  2.1 0.0 copy-start.5
  2.2 0.8 %copy-done.5 = bf16[64,256]{1,0:T(8,128)(2,1)S(1)} copy-done((bf16[64,256]{1,0:T(8,128)(2,1)S(1)}, bf16[64,256]{1,0:T(8,128)(2,1)}, u32[]{:S(2)}) %copy-start.5) | copy-done | bytes 32792
  2.9 0.0 copy-start.7
  2.9 0.8 %copy-done.7 = bf16[64,256]{1,0:T(8,128)(2,1)S(1)} copy-done((bf16[64,256]{1,0:T(8,128)(2,1)S(1)}, bf16[64,256]{1,0:T(8,128)(2,1)}, u32[]{:S(2)}) %copy-start.7) | copy-done | bytes 32792
  3.7 0.0 copy-start.8
  3.7 0.7 %copy-done.8 = f32[256]{0:T(256)S(1)} copy-done((f32[256]{0:T(256)S(1)}, f32[256]{0:T(256)}, u32[]{:S(2)}) %copy-start.8) | copy-done | bytes 1048
  4.3 0.1 shard_map.93
  4.4 0.0 copy-start.2
  4.4 0.0 copy-start.4
  4.4 0.0 copy-start.6
  4.5 27.5 %all_to_all.10.refs_1_ = f32[64,1,768]{2,1,0:T(1,128)S(1)} all-to-all(f32[64,1,768]{2,1,0:T(1,128)S(1)} %shard_map.93), channel_id=1, replica_groups={{0,4,8,12,16,20,24,28,32,36,40,44,48,52,56,60,64,68,72,76,80,84,88,92,9..., dimensions={0} | all-to-all | bytes 393216 | tf_op jit(solution)/shard_map/all_to_all | solution.py:158
  31.9 0.0 collective-permute-start
  31.9 1.4 %collective-permute-done.refs_2_ = f32[64,1,768]{2,1,0:T(1,128)S(1)} collective-permute-done((f32[64,1,768]{2,1,0:T(1,128)S(1)}, f32[64,1,768]{2,1,0:T(1,128)S(1)}, u32[]{:S(2)}, u32[]{:S(2)}) %collective-permute-start) | collective-permute-done | bytes 196640 | tf_op jit(solution)/shard_map/ppermute | solution.py:166
  33.4 0.0 copy-start
  33.4 1.4 %copy-done = bf16[11,256,256]{2,1,0:T(8,128)(2,1)S(1)} copy-done((bf16[11,256,256]{2,1,0:T(8,128)(2,1)S(1)}, bf16[11,256,256]{2,1,0:T(8,128)(2,1)}, u32[]{:S(2)}) %copy-start) | copy-done | bytes 1441816
  34.7 1.8 %shard_map.94 = f32[64,1,768]{2,1,0:T(1,128)S(1)} custom-call(s32[1]{0:T(128)} %bitcast.refs_0_, f32[64,1,768]{2,1,0:T(1,128)S(1)} %all_to_all.10.refs_1_, f32[64,1,768]{2,1,0:T(1,128)S(1)} %collective-permute-done.refs_2_, bf16[11,256,256]{2,1,0:T(8,128)(2,1)S(1)} %copy-done), custom_call_target="tpu_custom_call" | custom-call | tf_op jit(solution)/shard_map/pallas_call | solution.py:137
  36.6 18.2 %all_to_all.11.moved_ref = f32[64,1,768]{2,1,0:T(1,128)S(1)} all-to-all(f32[64,1,768]{2,1,0:T(1,128)S(1)} %shard_map.94), channel_id=1, replica_groups={{0,4,8,12,16,20,24,28,32,36,40,44,48,52,56,60,64,68,72,76,80,84,88,92,9..., dimensions={0} | all-to-all | bytes 393216 | tf_op jit(solution)/shard_map/all_to_all | solution.py:158
  54.9 0.7 %collective-permute-start.1 = (f32[256]{0:T(256)S(1)}, f32[256]{0:T(256)S(1)}, u32[]{:S(2)}, u32[]{:S(2)}) collective-permute-start(f32[256]{0:T(256)S(1)} %bitcast.3), channel_id=1, source_target_pairs={{0,1},{1,0},{2,3},{3,2},{4,5},{5,4},{6,7},{7,6},{8,9},{9,8},{10,11... | collective-permute-start | bytes 3080 | tf_op jit(solution)/shard_map/ppermute | solution.py:172
  55.5 0.0 copy-done.2
  55.5 0.0 copy-done.4
  55.5 0.0 copy-done.6
  55.5 0.7 %shard_map.95 = (bf16[64,256]{1,0:T(8,128)(2,1)}, bf16[64,256]{1,0:T(8,128)(2,1)}, bf16[64,256]{1,0:T(8,128)(2,1)}) custom-call(f32[64,1,768]{2,1,0:T(1,128)S(1)} %all_to_all.11.moved_ref, bf16[64,256]{1,0:T(8,128)(2,1)S(1)} %copy-done.2, bf16[64,256]{1,0:T(8,128)(2,1)S(1)} %copy-done.4, bf16[64,256]{1,0:T(8,128)(2,1)S(1)} %copy-done.6), custom_call_target="tpu_custom_call" | custom-call | tf_op jit(solution)/shard_map/pallas_call | solution.py:137
  56.2 2.3 %collective-permute-done.1 = f32[256]{0:T(256)S(1)} collective-permute-done((f32[256]{0:T(256)S(1)}, f32[256]{0:T(256)S(1)}, u32[]{:S(2)}, u32[]{:S(2)}) %collective-permute-start.1) | collective-permute-done | bytes 1056 | tf_op jit(solution)/shard_map/ppermute | solution.py:172
  58.5 0.6 add.8
  (1 shorter events, 0.0 us)
Async XLA Ops:
  0.6 0.8 %copy-start.1 = (bf16[64,256]{1,0:T(8,128)(2,1)S(1)}, bf16[64,256]{1,0:T(8,128)(2,1)}, u32[]{:S(2)}) copy-start(bf16[64,256]{1,0:T(8,128)(2,1)} %key_ref.3) | copy-start | bytes 98308
  1.4 0.8 %copy-start.3 = (bf16[64,256]{1,0:T(8,128)(2,1)S(1)}, bf16[64,256]{1,0:T(8,128)(2,1)}, u32[]{:S(2)}) copy-start(bf16[64,256]{1,0:T(8,128)(2,1)} %value_ref.3) | copy-start | bytes 98308
  2.1 0.8 %copy-start.5 = (bf16[64,256]{1,0:T(8,128)(2,1)S(1)}, bf16[64,256]{1,0:T(8,128)(2,1)}, u32[]{:S(2)}) copy-start(bf16[64,256]{1,0:T(8,128)(2,1)} %grad_ref.3) | copy-start | bytes 98308
  2.9 0.8 %copy-start.7 = (bf16[64,256]{1,0:T(8,128)(2,1)S(1)}, bf16[64,256]{1,0:T(8,128)(2,1)}, u32[]{:S(2)}) copy-start(bf16[64,256]{1,0:T(8,128)(2,1)} %query_ref.1) | copy-start | bytes 98308
  3.7 0.7 %copy-start.8 = (f32[256]{0:T(256)S(1)}, f32[256]{0:T(256)}, u32[]{:S(2)}) copy-start(f32[256]{0:T(256)} %param.9) | copy-start | bytes 3076
  4.4 51.1 %copy-start.2 = (bf16[64,256]{1,0:T(8,128)(2,1)S(1)}, bf16[64,256]{1,0:T(8,128)(2,1)}, u32[]{:S(2)}) copy-start(bf16[64,256]{1,0:T(8,128)(2,1)} %key_ref.3) | copy-start | bytes 98308
  4.4 51.1 %copy-start.4 = (bf16[64,256]{1,0:T(8,128)(2,1)S(1)}, bf16[64,256]{1,0:T(8,128)(2,1)}, u32[]{:S(2)}) copy-start(bf16[64,256]{1,0:T(8,128)(2,1)} %value_ref.3) | copy-start | bytes 98308
  4.4 51.1 %copy-start.6 = (bf16[64,256]{1,0:T(8,128)(2,1)S(1)}, bf16[64,256]{1,0:T(8,128)(2,1)}, u32[]{:S(2)}) copy-start(bf16[64,256]{1,0:T(8,128)(2,1)} %grad_ref.3) | copy-start | bytes 98308
  31.9 1.4 %collective-permute-start = (f32[64,1,768]{2,1,0:T(1,128)S(1)}, f32[64,1,768]{2,1,0:T(1,128)S(1)}, u32[]{:S(2)}, u32[]{:S(2)}) collective-permute-start(f32[64,1,768]{2,1,0:T(1,128)S(1)} %all_to_all.10.refs_1_), channel_id=1, source_target_pairs={{0,2},{2,0},{4,6},{6,4},{8,10},{10,8},{12,14},{14,12},{16,18},{18,... | collective-permute-start | bytes 589832 | tf_op jit(solution)/shard_map/ppermute | solution.py:166
  33.4 1.4 %copy-start = (bf16[11,256,256]{2,1,0:T(8,128)(2,1)S(1)}, bf16[11,256,256]{2,1,0:T(8,128)(2,1)}, u32[]{:S(2)}) copy-start(bf16[11,256,256]{2,1,0:T(8,128)(2,1)} %constant.21.clone.refs_3_) | copy-start | bytes 4325380
  54.9 3.7 %collective-permute-start.1 = (f32[256]{0:T(256)S(1)}, f32[256]{0:T(256)S(1)}, u32[]{:S(2)}, u32[]{:S(2)}) collective-permute-start(f32[256]{0:T(256)S(1)} %bitcast.3), channel_id=1, source_target_pairs={{0,1},{1,0},{2,3},{3,2},{4,5},{5,4},{6,7},{7,6},{8,9},{9,8},{10,11... | collective-permute-start | bytes 3080 | tf_op jit(solution)/shard_map/ppermute | solution.py:172

commit v3 on v2

--- a/solution.py
+++ b/solution.py
@@ -58,11 +58,31 @@
     return wide[:count] + wide[count:] + product(high, bank_ref[2 * odd + 1], transposed)
 
 
-def pack_body(query_ref, key_ref, value_ref, grad_ref, taps_ref, out_ref):
-    width = query_ref.shape[1]
-    out_ref[:, 0, :width] = key_ref[...].astype(jnp.float32) * value_ref[...].astype(jnp.float32)
-    out_ref[:, 0, width : 2 * width] = grad_ref[...].astype(jnp.float32) * query_ref[...].astype(jnp.float32)
-    out_ref[:, 0, 2 * width :] = jnp.broadcast_to(taps_ref[...], query_ref.shape)
+def fetch(pairs, arrived):
+    copies = [pltpu.make_async_copy(source, here, arrived.at[i]) for i, (source, here) in enumerate(pairs)]
+    for copy in copies:
+        copy.start()
+    return copies
+
+
+def pack_body(key_far, value_far, grad_far, query_far, taps_far, out_ref, key, value, grad, query, taps, arrived):
+    width = key.shape[1]
+    copies = fetch(
+        ((key_far, key), (value_far, value), (grad_far, grad), (query_far, query), (taps_far, taps)), arrived
+    )
+    copies[0].wait()
+    copies[1].wait()
+    out_ref[:, 0, :width] = key[...].astype(jnp.float32) * value[...].astype(jnp.float32)
+    copies[2].wait()
+    copies[3].wait()
+    out_ref[:, 0, width : 2 * width] = grad[...].astype(jnp.float32) * query[...].astype(jnp.float32)
+    copies[4].wait()
+    out_ref[:, 0, 2 * width :] = jnp.broadcast_to(taps[...], key.shape)
+
+
+def lead_body(own_ref, bank_far, bank_ref, arrived):
+    for copy in fetch([(bank_far, bank_ref)], arrived):
+        copy.wait()
 
 
 def middle_body(scale, parity_ref, own_ref, other_ref, bank_ref, out_ref):
@@ -70,9 +90,9 @@
     width = bank_ref.shape[2]
     half = width // 2
     rows = 2 * own_ref.shape[0]
-    high, low = split(jnp.concatenate([own_ref[:, 0, :], other_ref[:, 0, :]], axis=0))
     ahead = bank_ref[pl.ds(AHEAD + 2 * parity, 2)].reshape(2 * width, width)
-    front = product(ahead, jnp.concatenate([high, low], axis=0))
+    signal = jnp.concatenate([own_ref[:, 0, :], other_ref[:, 0, :]], axis=0)
+    front = product(ahead, jnp.concatenate(split(signal), axis=0))
     front = front[: 2 * rows] + front[2 * rows :]
     twist = [bank_ref[TWIST + i].astype(jnp.float32) for i in (0, 1)]
     cosine, sine = [table[:rows] + table[rows:] for table in twist]
@@ -123,22 +143,29 @@
     out_ref[...] = jnp.sum(moved_ref[:, 0, 2 * width :], axis=0, keepdims=True)
 
 
-def finish_body(moved_ref, key_ref, value_ref, grad_ref, query_out, key_out, value_out):
-    width = key_ref.shape[1]
-    conv = moved_ref[:, 0, :width]
+def finish_body(moved_ref, grad_far, value_far, key_far, query_out, key_out, value_out, grad, value, key, arrived):
+    width = key.shape[1]
+    copies = fetch(((grad_far, grad), (value_far, value), (key_far, key)), arrived)
     back = moved_ref[:, 0, width : 2 * width]
-    query_out[...] = (grad_ref[...].astype(jnp.float32) * conv).astype(jnp.bfloat16)
-    key_out[...] = (back * value_ref[...].astype(jnp.float32)).astype(jnp.bfloat16)
-    value_out[...] = (back * key_ref[...].astype(jnp.float32)).astype(jnp.bfloat16)
-
-
-def kernel_call(body, out_shape, limit, operands, in_specs=None):
-    placed = {} if in_specs is None else {"in_specs": in_specs}
+    copies[0].wait()
+    query_out[...] = (grad[...].astype(jnp.float32) * moved_ref[:, 0, :width]).astype(jnp.bfloat16)
+    copies[1].wait()
+    key_out[...] = (back * value[...].astype(jnp.float32)).astype(jnp.bfloat16)
+    copies[2].wait()
+    value_out[...] = (back * key[...].astype(jnp.float32)).astype(jnp.bfloat16)
+
+
+def add_body(left_ref, right_ref, out_ref):
+    out_ref[...] = left_ref[...] + right_ref[...]
+
+
+def kernel_call(body, out_shape, limit, operands, in_specs, scratch=()):
     return pl.pallas_call(
         body,
         out_shape=out_shape,
+        in_specs=in_specs,
+        scratch_shapes=scratch,
         compiler_params=pltpu.CompilerParams(vmem_limit_bytes=limit * MIB),
-        **placed,
     )(*operands)
 
 
@@ -160,20 +187,47 @@
     def middle(*refs):
         middle_body(scale, *refs)
 
-    taps = filter_taps.reshape(1, width)
-    packed = kernel_call(pack_body, message, 4, (query_proj, key_proj, value_proj, out_grad, taps))
+    far = pl.BlockSpec(memory_space=pltpu.HBM)
+    key_far, value_far, grad_far, query_far, taps_far = [
+        pltpu.with_memory_space_constraint(array, pltpu.HBM)
+        for array in (key_proj, value_proj, out_grad, query_proj, filter_taps.reshape(1, width))
+    ]
+    near = pl.BlockSpec(memory_space=pltpu.VMEM)
+    scalar = pl.BlockSpec(memory_space=pltpu.SMEM)
+    local = pltpu.VMEM((channels, width), jnp.bfloat16)
+    packed = kernel_call(
+        pack_body,
+        message,
+        4,
+        (key_far, value_far, grad_far, query_far, taps_far),
+        [far] * 5,
+        [local] * 4 + [pltpu.VMEM((1, width), jnp.float32), pltpu.SemaphoreType.DMA((5,))],
+    )
     own = exchange(packed)
     other = lax.ppermute(own, "ctx", other_core)
-    in_smem = pl.BlockSpec(memory_space=pltpu.SMEM)
-    in_vmem = pl.BlockSpec(memory_space=pltpu.VMEM)
-    restored = kernel_call(middle, message, 24, (parity, own, other, bank), [in_smem, in_vmem, in_vmem, in_vmem])
+    near_bank = kernel_call(
+        lead_body,
+        jax.ShapeDtypeStruct(bank.shape, bank.dtype),
+        8,
+        (own, pltpu.with_memory_space_constraint(bank, pltpu.HBM)),
+        [near, far],
+        [pltpu.SemaphoreType.DMA((1,))],
+    )
+    restored = kernel_call(middle, message, 24, (parity, own, other, near_bank), [scalar, near, near, near])
     moved = exchange(restored)
-    partial = kernel_call(sum_body, jax.ShapeDtypeStruct((1, width), jnp.float32), 4, (moved,)).reshape(width)
+    line = jax.ShapeDtypeStruct((1, width), jnp.float32)
+    partial = kernel_call(sum_body, line, 4, (moved,), [near])
     swapped = lax.ppermute(partial, "ch", [(0, 1), (1, 0)])
     query_grad, key_grad, value_grad = kernel_call(
-        finish_body, (narrow, narrow, narrow), 4, (moved, key_proj, value_proj, out_grad)
-    )
-    return (query_grad, key_grad, value_grad, partial + swapped)
+        finish_body,
+        (narrow, narrow, narrow),
+        4,
+        (moved, grad_far, value_far, key_far),
+        [near] + [far] * 3,
+        [local] * 3 + [pltpu.SemaphoreType.DMA((3,))],
+    )
+    filter_grad = kernel_call(add_body, line, 4, (partial, swapped), [near, near]).reshape(width)
+    return (query_grad, key_grad, value_grad, filter_grad)
 
 
 def solution(mesh):

time: 59.6 us -> 55.3 us (0.928)
  local copies, waits for them, and re-layouts: 5.08 us -> 0 us
  Pallas kernels: 2.62 us -> 6.17 us
  waiting for transfers between devices: 3.72 us -> 1.55 us
    unnamed x18 -> x0, local copies, waits for them, and re-layouts: 5.08 us -> none
    pallas_call x4 -> x6, Pallas kernels: 2.62 us -> 6.17 us  [kernel_call(): pl.pallas_call(body, out_shape=out_shape, in_specs=in_specs, scratch_shap...]
    ppermute x1, waiting for transfers between devices: 1.44 us -> 0.06 us  [shards(): other = lax.ppermute(own, 'ctx', other_core)]
    ppermute x1, waiting for transfers between devices: 2.29 us -> 1.49 us  [shards(): swapped = lax.ppermute(partial, 'ch', [(0, 1), (1, 0)])]
  transfers between devices with their start and end apart: 2 -> 2, of which waited for: 2 -> 2; matrix products, arithmetic and copies ran while one was open for 0% -> 0% of each run, Pallas kernels for 1% -> 5%
where the time goes in v3:
time: 55.3 us; the launch traced here: 55 us
  blocking collectives  45.9 us (83%)
  Pallas kernels  6.17 us (11%)
  waiting for transfers between devices  1.55 us (3%)
  starting transfers between devices  0.68 us (1%)
  between operations  0.67 us (1%)
    all_to_all x2, blocking collectives, exchange(): lax.all_to_all(array, 'ctx', 0, 0, axis_index_groups=same_core, tiled=True)  45.9 us
    pallas_call x6, Pallas kernels, kernel_call(): pl.pallas_call(body, out_shape=out_shape, in_specs=in_specs, scratch_shap...  6.17 us
    ppermute x1, waiting for transfers between devices, shards(): swapped = lax.ppermute(partial, 'ch', [(0, 1), (1, 0)])  1.49 us
  transfers between devices with their start and end apart: 2, of which 2 were waited for; matrix products, arithmetic and copies ran while one was open for 0% of the time, Pallas kernels for 5%

profile of v3, /device:TPU:32, one launch (start us, length us, event | category | flops | bytes accessed | tf_op | source)
XLA Modules:
  0.0 55.0 jit_solution(16632473173652963874)
XLA Ops:
  0.6 0.9 %shard_map.93 = f32[64,1,768]{2,1,0:T(1,128)S(1)} custom-call(bf16[64,256]{1,0:T(8,128)(2,1)} %key_far.3, bf16[64,256]{1,0:T(8,128)(2,1)} %value_far.3, bf16[64,256]{1,0:T(8,128)(2,1)} %grad_far.3, bf16[64,256]{1,0:T(8,128)(2,1)} %query_far.1, f32[1,256]{1,0:T(1,128)} %bitcast.3), custom_call_target="tpu_custom_call" | custom-call | tf_op jit(solution)/shard_map/pallas_call | solution.py:163
  1.5 27.3 %all_to_all.10.own_ref.refs_1_ = f32[64,1,768]{2,1,0:T(1,128)S(1)} all-to-all(f32[64,1,768]{2,1,0:T(1,128)S(1)} %shard_map.93), channel_id=1, replica_groups={{0,4,8,12,16,20,24,28,32,36,40,44,48,52,56,60,64,68,72,76,80,84,88,92,9..., dimensions={0} | all-to-all | bytes 393216 | tf_op jit(solution)/shard_map/all_to_all | solution.py:185
  28.9 0.0 collective-permute-start
  28.9 1.4 %shard_map.94.refs_3_ = bf16[11,256,256]{2,1,0:T(8,128)(2,1)S(1)} custom-call(f32[64,1,768]{2,1,0:T(1,128)S(1)} %all_to_all.10.own_ref.refs_1_, bf16[11,256,256]{2,1,0:T(8,128)(2,1)} %constant.21.clone.bank_far), custom_call_target="tpu_custom_call" | custom-call | tf_op jit(solution)/shard_map/pallas_call | solution.py:163
  30.3 0.1 collective-permute-done.refs_2_
  30.3 1.8 %shard_map.95 = f32[64,1,768]{2,1,0:T(1,128)S(1)} custom-call(s32[1]{0:T(128)} %bitcast.refs_0_, f32[64,1,768]{2,1,0:T(1,128)S(1)} %all_to_all.10.own_ref.refs_1_, f32[64,1,768]{2,1,0:T(1,128)S(1)} %collective-permute-done.refs_2_, bf16[11,256,256]{2,1,0:T(8,128)(2,1)S(1)} %shard_map.94.refs_3_), custom_call_target="tpu_custom_call" | custom-call | tf_op jit(solution)/shard_map/pallas_call | solution.py:163
  32.1 18.6 %all_to_all.11.moved_ref = f32[64,1,768]{2,1,0:T(1,128)S(1)} all-to-all(f32[64,1,768]{2,1,0:T(1,128)S(1)} %shard_map.95), channel_id=1, replica_groups={{0,4,8,12,16,20,24,28,32,36,40,44,48,52,56,60,64,68,72,76,80,84,88,92,9..., dimensions={0} | all-to-all | bytes 393216 | tf_op jit(solution)/shard_map/all_to_all | solution.py:185
  50.8 0.7 %collective-permute-start.1 = (f32[1,256]{1,0:T(1,128)S(1)}, f32[1,256]{1,0:T(1,128)S(1)}, u32[]{:S(2)}, u32[]{:S(2)}) collective-permute-start(f32[1,256]{1,0:T(1,128)S(1)} %shard_map.97.left_ref), channel_id=1, source_target_pairs={{0,1},{1,0},{2,3},{3,2},{4,5},{5,4},{6,7},{7,6},{8,9},{9,8},{10,11... | collective-permute-start | bytes 3080 | tf_op jit(solution)/shard_map/ppermute | solution.py:220
  51.4 1.5 %shard_map.96 = (bf16[64,256]{1,0:T(8,128)(2,1)}, bf16[64,256]{1,0:T(8,128)(2,1)}, bf16[64,256]{1,0:T(8,128)(2,1)}) custom-call(f32[64,1,768]{2,1,0:T(1,128)S(1)} %all_to_all.11.moved_ref, bf16[64,256]{1,0:T(8,128)(2,1)} %grad_far.3, bf16[64,256]{1,0:T(8,128)(2,1)} %value_far.3, bf16[64,256]{1,0:T(8,128)(2,1)} %key_far.3), custom_call_target="tpu_custom_call" | custom-call | tf_op jit(solution)/shard_map/pallas_call | solution.py:163
  52.9 1.5 %collective-permute-done.1.right_ref = f32[1,256]{1,0:T(1,128)S(1)} collective-permute-done((f32[1,256]{1,0:T(1,128)S(1)}, f32[1,256]{1,0:T(1,128)S(1)}, u32[]{:S(2)}, u32[]{:S(2)}) %collective-permute-start.1) | collective-permute-done | bytes 1056 | tf_op jit(solution)/shard_map/ppermute | solution.py:220
  54.4 0.6 %shard_map.98 = f32[1,256]{1,0:T(1,128)} custom-call(f32[1,256]{1,0:T(1,128)S(1)} %shard_map.97.left_ref, f32[1,256]{1,0:T(1,128)S(1)} %collective-permute-done.1.right_ref), custom_call_target="tpu_custom_call" | custom-call | tf_op jit(solution)/shard_map/pallas_call | solution.py:163
  (1 shorter events, 0.0 us)
Async XLA Ops:
  28.9 1.4 %collective-permute-start = (f32[64,1,768]{2,1,0:T(1,128)S(1)}, f32[64,1,768]{2,1,0:T(1,128)S(1)}, u32[]{:S(2)}, u32[]{:S(2)}) collective-permute-start(f32[64,1,768]{2,1,0:T(1,128)S(1)} %all_to_all.10.own_ref.refs_1_), channel_id=1, source_target_pairs={{0,2},{2,0},{4,6},{6,4},{8,10},{10,8},{12,14},{14,12},{16,18},{18,... | collective-permute-start | bytes 589832 | tf_op jit(solution)/shard_map/ppermute | solution.py:207
  50.8 3.7 %collective-permute-start.1 = (f32[1,256]{1,0:T(1,128)S(1)}, f32[1,256]{1,0:T(1,128)S(1)}, u32[]{:S(2)}, u32[]{:S(2)}) collective-permute-start(f32[1,256]{1,0:T(1,128)S(1)} %shard_map.97.left_ref), channel_id=1, source_target_pairs={{0,1},{1,0},{2,3},{3,2},{4,5},{5,4},{6,7},{7,6},{8,9},{9,8},{10,11... | collective-permute-start | bytes 3080 | tf_op jit(solution)/shard_map/ppermute | solution.py:220

commit v4 on v3

--- a/solution.py
+++ b/solution.py
@@ -10,6 +10,7 @@
 
 SHIFT = 0.25
 MIB = 1024 * 1024
+ORDER = np.roll(np.arange(64), -((1 * 8 + 4) * 4 + 2))
 AHEAD, BACK, TWIST = 4, 8, 9
 
 
@@ -30,7 +31,7 @@
         planes += halves(np.block([[cosine, -sine], [sine, cosine]]))
     block_angle = 2.0 * math.pi * np.outer(rows, np.arange(blocks)) / blocks
     block_table = np.concatenate([np.cos(block_angle), -np.sin(block_angle)], axis=0)
-    own = [np.arange(parity, blocks, 2) for parity in (0, 1)]
+    own = [2 * ORDER + parity for parity in (0, 1)]
     for e in (0, 1):
         high, low = halves(np.concatenate([block_table[:, own[e]], block_table[:, own[1 - e]]], axis=1))
         planes += [np.concatenate([high, high], axis=1), np.concatenate([low, np.zeros_like(low)], axis=1)]
@@ -174,7 +175,7 @@
     channels, width = query_proj.shape
     chips = devices // 2
     parity = (lax.axis_index("ctx") % 2).astype(jnp.int32).reshape(1)
-    same_core = [[2 * chip + core for chip in range(chips)] for core in (0, 1)]
+    same_core = [[int(2 * chip + core) for chip in ORDER] for core in (0, 1)]
     other_core = [(device, device ^ 1) for device in range(devices)]
     scale = 1.0 / math.sqrt(channels * lax.axis_size("ch") * devices * width)
     message = jax.ShapeDtypeStruct((chips, 1, 3 * width), jnp.float32)

time: 55.3 us -> 50.1 us (0.906)
  the two profiles are of different devices: /device:TPU:32 before, /device:TPU:6 now
where the time goes in v4:
time: 50.1 us; the launch traced here: 49.7 us
  blocking collectives  40.7 us (81%)
  Pallas kernels  6.17 us (12%)
  waiting for transfers between devices  2.12 us (4%)
  between operations  0.67 us (1%)
    all_to_all x2, blocking collectives, exchange(): lax.all_to_all(array, 'ctx', 0, 0, axis_index_groups=same_core, tiled=True)  40.7 us
    pallas_call x6, Pallas kernels, kernel_call(): pl.pallas_call(body, out_shape=out_shape, in_specs=in_specs, scratch_shap...  6.17 us
    ppermute x1, waiting for transfers between devices, shards(): swapped = lax.ppermute(partial, 'ch', [(0, 1), (1, 0)])  2.06 us
  transfers between devices with their start and end apart: 2, of which 2 were waited for; matrix products, arithmetic and copies ran while one was open for 0% of the time, Pallas kernels for 6%

profile of v4, /device:TPU:6, one launch (start us, length us, event | category | flops | bytes accessed | tf_op | source)
XLA Modules:
  0.0 49.7 jit_solution(6273038284861378549)
XLA Ops:
  0.6 0.9 %shard_map.93 = f32[64,1,768]{2,1,0:T(1,128)S(1)} custom-call(bf16[64,256]{1,0:T(8,128)(2,1)} %key_far.3, bf16[64,256]{1,0:T(8,128)(2,1)} %value_far.3, bf16[64,256]{1,0:T(8,128)(2,1)} %grad_far.3, bf16[64,256]{1,0:T(8,128)(2,1)} %query_far.1, f32[1,256]{1,0:T(1,128)} %bitcast.3), custom_call_target="tpu_custom_call" | custom-call | tf_op jit(solution)/shard_map/pallas_call | solution.py:164
  1.5 22.2 %all_to_all.10.own_ref.refs_1_ = f32[64,1,768]{2,1,0:T(1,128)S(1)} all-to-all(f32[64,1,768]{2,1,0:T(1,128)S(1)} %shard_map.93), channel_id=1, replica_groups={{200,204,208,212,216,220,224,228,232,236,240,244,248,252,0,4,8,12,16,20..., dimensions={0} | all-to-all | bytes 393216 | tf_op jit(solution)/shard_map/all_to_all | solution.py:186
  23.7 0.0 collective-permute-start
  23.7 1.4 %shard_map.94.refs_3_ = bf16[11,256,256]{2,1,0:T(8,128)(2,1)S(1)} custom-call(f32[64,1,768]{2,1,0:T(1,128)S(1)} %all_to_all.10.own_ref.refs_1_, bf16[11,256,256]{2,1,0:T(8,128)(2,1)} %constant.21.clone.bank_far), custom_call_target="tpu_custom_call" | custom-call | tf_op jit(solution)/shard_map/pallas_call | solution.py:164
  25.1 0.1 collective-permute-done.refs_2_
  25.2 1.8 %shard_map.95 = f32[64,1,768]{2,1,0:T(1,128)S(1)} custom-call(s32[1]{0:T(128)} %bitcast.refs_0_, f32[64,1,768]{2,1,0:T(1,128)S(1)} %all_to_all.10.own_ref.refs_1_, f32[64,1,768]{2,1,0:T(1,128)S(1)} %collective-permute-done.refs_2_, bf16[11,256,256]{2,1,0:T(8,128)(2,1)S(1)} %shard_map.94.refs_3_), custom_call_target="tpu_custom_call" | custom-call | tf_op jit(solution)/shard_map/pallas_call | solution.py:164
  27.0 18.5 %all_to_all.11.moved_ref = f32[64,1,768]{2,1,0:T(1,128)S(1)} all-to-all(f32[64,1,768]{2,1,0:T(1,128)S(1)} %shard_map.95), channel_id=1, replica_groups={{200,204,208,212,216,220,224,228,232,236,240,244,248,252,0,4,8,12,16,20..., dimensions={0} | all-to-all | bytes 393216 | tf_op jit(solution)/shard_map/all_to_all | solution.py:186
  45.5 0.1 collective-permute-start.1
  45.6 1.5 %shard_map.96 = (bf16[64,256]{1,0:T(8,128)(2,1)}, bf16[64,256]{1,0:T(8,128)(2,1)}, bf16[64,256]{1,0:T(8,128)(2,1)}) custom-call(f32[64,1,768]{2,1,0:T(1,128)S(1)} %all_to_all.11.moved_ref, bf16[64,256]{1,0:T(8,128)(2,1)} %grad_far.3, bf16[64,256]{1,0:T(8,128)(2,1)} %value_far.3, bf16[64,256]{1,0:T(8,128)(2,1)} %key_far.3), custom_call_target="tpu_custom_call" | custom-call | tf_op jit(solution)/shard_map/pallas_call | solution.py:164
  47.1 2.1 %collective-permute-done.1.right_ref = f32[1,256]{1,0:T(1,128)S(1)} collective-permute-done((f32[1,256]{1,0:T(1,128)S(1)}, f32[1,256]{1,0:T(1,128)S(1)}, u32[]{:S(2)}, u32[]{:S(2)}) %collective-permute-start.1) | collective-permute-done | bytes 1056 | tf_op jit(solution)/shard_map/ppermute | solution.py:221
  49.2 0.6 %shard_map.98 = f32[1,256]{1,0:T(1,128)} custom-call(f32[1,256]{1,0:T(1,128)S(1)} %shard_map.97.left_ref, f32[1,256]{1,0:T(1,128)S(1)} %collective-permute-done.1.right_ref), custom_call_target="tpu_custom_call" | custom-call | tf_op jit(solution)/shard_map/pallas_call | solution.py:164
  (1 shorter events, 0.0 us)
Async XLA Ops:
  23.7 1.4 %collective-permute-start = (f32[64,1,768]{2,1,0:T(1,128)S(1)}, f32[64,1,768]{2,1,0:T(1,128)S(1)}, u32[]{:S(2)}, u32[]{:S(2)}) collective-permute-start(f32[64,1,768]{2,1,0:T(1,128)S(1)} %all_to_all.10.own_ref.refs_1_), channel_id=1, source_target_pairs={{0,2},{2,0},{4,6},{6,4},{8,10},{10,8},{12,14},{14,12},{16,18},{18,... | collective-permute-start | bytes 589832 | tf_op jit(solution)/shard_map/ppermute | solution.py:208
  45.5 3.7 %collective-permute-start.1 = (f32[1,256]{1,0:T(1,128)S(1)}, f32[1,256]{1,0:T(1,128)S(1)}, u32[]{:S(2)}, u32[]{:S(2)}) collective-permute-start(f32[1,256]{1,0:T(1,128)S(1)} %shard_map.97.left_ref), channel_id=1, source_target_pairs={{0,1},{1,0},{2,3},{3,2},{4,5},{5,4},{6,7},{7,6},{8,9},{9,8},{10,11... | collective-permute-start | bytes 3080 | tf_op jit(solution)/shard_map/ppermute | solution.py:221

commit v5 on v4

--- a/solution.py
+++ b/solution.py
@@ -10,7 +10,7 @@
 
 SHIFT = 0.25
 MIB = 1024 * 1024
-ORDER = np.roll(np.arange(64), -((1 * 8 + 4) * 4 + 2))
+ORDER = np.array([((1 - x) * 8 + (4 + 3 * z) % 8) * 4 + (2 + y) % 4 for z in range(8) for y in range(4) for x in range(2)])
 AHEAD, BACK, TWIST = 4, 8, 9
 
 
@@ -144,16 +144,12 @@
     out_ref[...] = jnp.sum(moved_ref[:, 0, 2 * width :], axis=0, keepdims=True)
 
 
-def finish_body(moved_ref, grad_far, value_far, key_far, query_out, key_out, value_out, grad, value, key, arrived):
-    width = key.shape[1]
-    copies = fetch(((grad_far, grad), (value_far, value), (key_far, key)), arrived)
+def finish_body(moved_ref, key_ref, value_ref, grad_ref, query_out, key_out, value_out):
+    width = key_ref.shape[1]
     back = moved_ref[:, 0, width : 2 * width]
-    copies[0].wait()
-    query_out[...] = (grad[...].astype(jnp.float32) * moved_ref[:, 0, :width]).astype(jnp.bfloat16)
-    copies[1].wait()
-    key_out[...] = (back * value[...].astype(jnp.float32)).astype(jnp.bfloat16)
-    copies[2].wait()
-    value_out[...] = (back * key[...].astype(jnp.float32)).astype(jnp.bfloat16)
+    query_out[...] = (grad_ref[...].astype(jnp.float32) * moved_ref[:, 0, :width]).astype(jnp.bfloat16)
+    key_out[...] = (back * value_ref[...].astype(jnp.float32)).astype(jnp.bfloat16)
+    value_out[...] = (back * key_ref[...].astype(jnp.float32)).astype(jnp.bfloat16)
 
 
 def add_body(left_ref, right_ref, out_ref):
@@ -196,13 +192,13 @@
     near = pl.BlockSpec(memory_space=pltpu.VMEM)
     scalar = pl.BlockSpec(memory_space=pltpu.SMEM)
     local = pltpu.VMEM((channels, width), jnp.bfloat16)
-    packed = kernel_call(
+    packed, key, value, grad = kernel_call(
         pack_body,
-        message,
+        (message, narrow, narrow, narrow),
         4,
         (key_far, value_far, grad_far, query_far, taps_far),
         [far] * 5,
-        [local] * 4 + [pltpu.VMEM((1, width), jnp.float32), pltpu.SemaphoreType.DMA((5,))],
+        [local, pltpu.VMEM((1, width), jnp.float32), pltpu.SemaphoreType.DMA((5,))],
     )
     own = exchange(packed)
     other = lax.ppermute(own, "ctx", other_core)
@@ -220,12 +216,7 @@
     partial = kernel_call(sum_body, line, 4, (moved,), [near])
     swapped = lax.ppermute(partial, "ch", [(0, 1), (1, 0)])
     query_grad, key_grad, value_grad = kernel_call(
-        finish_body,
-        (narrow, narrow, narrow),
-        4,
-        (moved, grad_far, value_far, key_far),
-        [near] + [far] * 3,
-        [local] * 3 + [pltpu.SemaphoreType.DMA((3,))],
+        finish_body, (narrow, narrow, narrow), 4, (moved, key, value, grad), [near] * 4
     )
     filter_grad = kernel_call(add_body, line, 4, (partial, swapped), [near, near]).reshape(width)
     return (query_grad, key_grad, value_grad, filter_grad)

time: 50.1 us -> 49.7 us (level)
  waiting for transfers between devices: 2.12 us -> 2.94 us
  Pallas kernels: 6.17 us -> 5.37 us
    ppermute x1, waiting for transfers between devices: 2.06 us -> 2.87 us  [shards(): swapped = lax.ppermute(partial, 'ch', [(0, 1), (1, 0)])]
    pallas_call x6, Pallas kernels: 6.17 us -> 5.37 us  [kernel_call(): pl.pallas_call(body, out_shape=out_shape, in_specs=in_specs, scratch_shap...]
  transfers between devices with their start and end apart: 2 -> 2, of which waited for: 2 -> 2; matrix products, arithmetic and copies ran while one was open for 0% -> 0% of each run, Pallas kernels for 6% -> 4%
where the time goes in v5:
time: 49.7 us; the launch traced here: 49.5 us
  blocking collectives  40.4 us (81%)
  Pallas kernels  5.37 us (11%)
  waiting for transfers between devices  2.94 us (6%)
  between operations  0.67 us (1%)
    all_to_all x2, blocking collectives, exchange(): lax.all_to_all(array, 'ctx', 0, 0, axis_index_groups=same_core, tiled=True)  40.4 us
    pallas_call x6, Pallas kernels, kernel_call(): pl.pallas_call(body, out_shape=out_shape, in_specs=in_specs, scratch_shap...  5.37 us
    ppermute x1, waiting for transfers between devices, shards(): swapped = lax.ppermute(partial, 'ch', [(0, 1), (1, 0)])  2.87 us
  transfers between devices with their start and end apart: 2, of which 2 were waited for; matrix products, arithmetic and copies ran while one was open for 0% of the time, Pallas kernels for 4%

profile of v5, /device:TPU:6, one launch (start us, length us, event | category | flops | bytes accessed | tf_op | source)
XLA Modules:
  0.0 49.5 jit_solution(16067574403061085004)
XLA Ops:
  0.6 0.9 %shard_map.93 = (f32[64,1,768]{2,1,0:T(1,128)S(1)}, bf16[64,256]{1,0:T(8,128)(2,1)S(1)}, bf16[64,256]{1,0:T(8,128)(2,1)S(1)}, bf16[64,256]{1,0:T(8,128)(2,1)S(1)}) custom-call(bf16[64,256]{1,0:T(8,128)(2,1)} %key_far.1, bf16[64,256]{1,0:T(8,128)(2,1)} %value_far.1, bf16[64,256]{1,0:T(8,128)(2,1)} %grad_far.1, bf16[64,256]{1,0:T(8,128)(2,1)} %query_far.1, ...), custom_call_target="tpu_custom_call" | custom-call | tf_op jit(solution)/shard_map/pallas_call | solution.py:160
  1.5 22.0 %all_to_all.10.own_ref.refs_1_ = f32[64,1,768]{2,1,0:T(1,128)S(1)} all-to-all(f32[64,1,768]{2,1,0:T(1,128)S(1)} %get-tuple-element.11), channel_id=1, replica_groups={{200,72,204,76,192,64,196,68,248,120,252,124,240,112,244,116,168,40,172..., dimensions={0} | all-to-all | bytes 393216 | tf_op jit(solution)/shard_map/all_to_all | solution.py:182
  23.6 0.0 collective-permute-start
  23.6 1.4 %shard_map.94.refs_3_ = bf16[11,256,256]{2,1,0:T(8,128)(2,1)S(1)} custom-call(f32[64,1,768]{2,1,0:T(1,128)S(1)} %all_to_all.10.own_ref.refs_1_, bf16[11,256,256]{2,1,0:T(8,128)(2,1)} %constant.21.clone.bank_far), custom_call_target="tpu_custom_call" | custom-call | tf_op jit(solution)/shard_map/pallas_call | solution.py:160
  24.9 0.1 collective-permute-done.refs_2_
  25.0 1.8 %shard_map.95 = f32[64,1,768]{2,1,0:T(1,128)S(1)} custom-call(s32[1]{0:T(128)} %bitcast.refs_0_, f32[64,1,768]{2,1,0:T(1,128)S(1)} %all_to_all.10.own_ref.refs_1_, f32[64,1,768]{2,1,0:T(1,128)S(1)} %collective-permute-done.refs_2_, bf16[11,256,256]{2,1,0:T(8,128)(2,1)S(1)} %shard_map.94.refs_3_), custom_call_target="tpu_custom_call" | custom-call | tf_op jit(solution)/shard_map/pallas_call | solution.py:160
  26.8 18.4 %all_to_all.11.moved_ref = f32[64,1,768]{2,1,0:T(1,128)S(1)} all-to-all(f32[64,1,768]{2,1,0:T(1,128)S(1)} %shard_map.95), channel_id=1, replica_groups={{200,72,204,76,192,64,196,68,248,120,252,124,240,112,244,116,168,40,172..., dimensions={0} | all-to-all | bytes 393216 | tf_op jit(solution)/shard_map/all_to_all | solution.py:182
  45.2 0.1 collective-permute-start.1
  45.3 0.7 %shard_map.96 = (bf16[64,256]{1,0:T(8,128)(2,1)}, bf16[64,256]{1,0:T(8,128)(2,1)}, bf16[64,256]{1,0:T(8,128)(2,1)}) custom-call(f32[64,1,768]{2,1,0:T(1,128)S(1)} %all_to_all.11.moved_ref, bf16[64,256]{1,0:T(8,128)(2,1)S(1)} %get-tuple-element.12.key_ref, bf16[64,256]{1,0:T(8,128)(2,1)S(1)} %get-tuple-element.13.value_ref, ...), custom_call_target="tpu_custom_call" | custom-call | tf_op jit(solution)/shard_map/pallas_call | solution.py:160
  46.0 2.9 %collective-permute-done.1.right_ref = f32[1,256]{1,0:T(1,128)S(1)} collective-permute-done((f32[1,256]{1,0:T(1,128)S(1)}, f32[1,256]{1,0:T(1,128)S(1)}, u32[]{:S(2)}, u32[]{:S(2)}) %collective-permute-start.1) | collective-permute-done | bytes 1056 | tf_op jit(solution)/shard_map/ppermute | solution.py:217
  48.9 0.6 %shard_map.98 = f32[1,256]{1,0:T(1,128)} custom-call(f32[1,256]{1,0:T(1,128)S(1)} %shard_map.97.left_ref, f32[1,256]{1,0:T(1,128)S(1)} %collective-permute-done.1.right_ref), custom_call_target="tpu_custom_call" | custom-call | tf_op jit(solution)/shard_map/pallas_call | solution.py:160
  (1 shorter events, 0.0 us)
Async XLA Ops:
  23.6 1.4 %collective-permute-start = (f32[64,1,768]{2,1,0:T(1,128)S(1)}, f32[64,1,768]{2,1,0:T(1,128)S(1)}, u32[]{:S(2)}, u32[]{:S(2)}) collective-permute-start(f32[64,1,768]{2,1,0:T(1,128)S(1)} %all_to_all.10.own_ref.refs_1_), channel_id=1, source_target_pairs={{0,2},{2,0},{4,6},{6,4},{8,10},{10,8},{12,14},{14,12},{16,18},{18,... | collective-permute-start | bytes 589832 | tf_op jit(solution)/shard_map/ppermute | solution.py:204
  45.2 3.7 %collective-permute-start.1 = (f32[1,256]{1,0:T(1,128)S(1)}, f32[1,256]{1,0:T(1,128)S(1)}, u32[]{:S(2)}, u32[]{:S(2)}) collective-permute-start(f32[1,256]{1,0:T(1,128)S(1)} %shard_map.97.left_ref), channel_id=1, source_target_pairs={{0,1},{1,0},{2,3},{3,2},{4,5},{5,4},{6,7},{7,6},{8,9},{9,8},{10,11... | collective-permute-start | bytes 3080 | tf_op jit(solution)/shard_map/ppermute | solution.py:217

commit v6 on v5

--- a/solution.py
+++ b/solution.py
@@ -10,6 +10,7 @@
 
 SHIFT = 0.25
 MIB = 1024 * 1024
+PARTS = 2
 ORDER = np.array([((1 - x) * 8 + (4 + 3 * z) % 8) * 4 + (2 + y) % 4 for z in range(8) for y in range(4) for x in range(2)])
 AHEAD, BACK, TWIST = 4, 8, 9
 
@@ -93,30 +94,44 @@
     rows = 2 * own_ref.shape[0]
     ahead = bank_ref[pl.ds(AHEAD + 2 * parity, 2)].reshape(2 * width, width)
     signal = jnp.concatenate([own_ref[:, 0, :], other_ref[:, 0, :]], axis=0)
-    front = product(ahead, jnp.concatenate(split(signal), axis=0))
-    front = front[: 2 * rows] + front[2 * rows :]
+    data = jnp.concatenate(split(signal), axis=0)
+    fronts = []
+    for index in range(3):
+        wide = product(ahead, data[:, index * width : (index + 1) * width])
+        fronts.append(wide[: 2 * rows] + wide[2 * rows :])
     twist = [bank_ref[TWIST + i].astype(jnp.float32) for i in (0, 1)]
     cosine, sine = [table[:rows] + table[rows:] for table in twist]
-    even, odd = [], []
-    for index in range(3):
-        real = front[:rows, index * width : (index + 1) * width]
-        imag = front[rows:, index * width : (index + 1) * width]
-        real, imag = real * cosine + imag * sine, imag * cosine - real * sine
-        even.append(jnp.concatenate([real[:, :half] + real[:, half:], imag[:, :half] + imag[:, half:]], axis=1))
-        odd.append(jnp.concatenate([real[:, :half] - real[:, half:], imag[:, :half] - imag[:, half:]], axis=1))
-    waves = []
-    for bins, stacked in enumerate((even, odd)):
-        spectra = inner_product(jnp.concatenate(stacked, axis=0), bank_ref, bins, False)
-        gated_real, gated_imag = spectra[:rows, :half], spectra[:rows, half:]
-        grad_real, grad_imag = spectra[rows : 2 * rows, :half], spectra[rows : 2 * rows, half:]
-        taps_real, taps_imag = spectra[2 * rows :, :half], spectra[2 * rows :, half:]
+    reals = [[] for _ in range(3)]
+    imags = [[] for _ in range(3)]
+    size = rows // PARTS
+    stacks, spectras, mixes, outs = {}, {}, {}, {}
+    pieces = [(part, bins) for bins in (0, 1) for part in range(PARTS)]
+
+    def twisted(part):
+        here = slice(part * size, (part + 1) * size)
+        there = slice(rows + part * size, rows + (part + 1) * size)
+        even, odd = [], []
+        for index in range(3):
+            real = fronts[index][here]
+            imag = fronts[index][there]
+            real, imag = real * cosine[here] + imag * sine[here], imag * cosine[here] - real * sine[here]
+            even.append(jnp.concatenate([real[:, :half] + real[:, half:], imag[:, :half] + imag[:, half:]], axis=1))
+            odd.append(jnp.concatenate([real[:, :half] - real[:, half:], imag[:, :half] - imag[:, half:]], axis=1))
+        stacks[part, 0] = jnp.concatenate(even, axis=0)
+        stacks[part, 1] = jnp.concatenate(odd, axis=0)
+
+    def mix(key):
+        spectra = spectras[key]
+        gated_real, gated_imag = spectra[:size, :half], spectra[:size, half:]
+        grad_real, grad_imag = spectra[size : 2 * size, :half], spectra[size : 2 * size, half:]
+        taps_real, taps_imag = spectra[2 * size :, :half], spectra[2 * size :, half:]
         conv_real = gated_real * taps_real - gated_imag * taps_imag
         conv_imag = gated_real * taps_imag + gated_imag * taps_real
         back_real = grad_real * taps_real + grad_imag * taps_imag
         back_imag = grad_imag * taps_real - grad_real * taps_imag
         cross_real = (grad_real * gated_real + grad_imag * gated_imag) * scale
         cross_imag = (grad_imag * gated_real - grad_real * gated_imag) * scale
-        mixed = jnp.concatenate(
+        mixes[key] = jnp.concatenate(
             [
                 jnp.concatenate([conv_real, conv_imag], axis=1),
                 jnp.concatenate([back_real, back_imag], axis=1),
@@ -124,19 +139,35 @@
             ],
             axis=0,
         )
-        waves.append(inner_product(mixed, bank_ref, bins, True))
-    turned = []
+
+    def untwist(part):
+        here = slice(part * size, (part + 1) * size)
+        for index in range(3):
+            first = outs[part, 0][index * size : (index + 1) * size]
+            second = outs[part, 1][index * size : (index + 1) * size]
+            total, difference = first + second, first - second
+            real = jnp.concatenate([total[:, :half], difference[:, :half]], axis=1)
+            imag = jnp.concatenate([total[:, half:], difference[:, half:]], axis=1)
+            reals[index].append(real * cosine[here] - imag * sine[here])
+            imags[index].append(real * sine[here] + imag * cosine[here])
+
+    for part in range(PARTS):
+        twisted(part)
+    for key in pieces:
+        spectras[key] = inner_product(stacks[key], bank_ref, key[1], False)
+    for key in pieces:
+        mix(key)
+    for key in pieces:
+        outs[key] = inner_product(mixes[key], bank_ref, key[1], True)
+    for part in range(PARTS):
+        untwist(part)
+    table = bank_ref[BACK, pl.ds(pl.multiple_of(rows * parity, rows), rows)]
     for index in range(3):
-        first = waves[0][index * rows : (index + 1) * rows]
-        second = waves[1][index * rows : (index + 1) * rows]
-        total, difference = first + second, first - second
-        real = jnp.concatenate([total[:, :half], difference[:, :half]], axis=1)
-        imag = jnp.concatenate([total[:, half:], difference[:, half:]], axis=1)
-        turned.append(jnp.concatenate([real * cosine - imag * sine, real * sine + imag * cosine], axis=0))
-    high, low = split(jnp.concatenate(turned, axis=1))
-    table = bank_ref[BACK, pl.ds(pl.multiple_of(rows * parity, rows), rows)]
-    wide = product(table, high)
-    out_ref[:, 0, :] = wide[: rows // 2] + wide[rows // 2 :] + product(table[: rows // 2], low)
+        high, low = split(jnp.concatenate(reals[index] + imags[index], axis=0))
+        wide = product(table, high)
+        out_ref[:, 0, index * width : (index + 1) * width] = (
+            wide[: rows // 2] + wide[rows // 2 :] + product(table[: rows // 2], low)
+        )
 
 
 def sum_body(moved_ref, out_ref):

time: 49.7 us -> 49.4 us (level)
  no operation moved by 1% of the time
where the time goes in v6:
time: 49.4 us; the launch traced here: 49.2 us
  blocking collectives  40.4 us (82%)
  Pallas kernels  5.05 us (10%)
  waiting for transfers between devices  2.94 us (6%)
  between operations  0.67 us (1%)
    all_to_all x2, blocking collectives, exchange(): lax.all_to_all(array, 'ctx', 0, 0, axis_index_groups=same_core, tiled=True)  40.4 us
    pallas_call x6, Pallas kernels, kernel_call(): pl.pallas_call(body, out_shape=out_shape, in_specs=in_specs, scratch_shap...  5.05 us
    ppermute x1, waiting for transfers between devices, shards(): swapped = lax.ppermute(partial, 'ch', [(0, 1), (1, 0)])  2.87 us
  transfers between devices with their start and end apart: 2, of which 2 were waited for; matrix products, arithmetic and copies ran while one was open for 0% of the time, Pallas kernels for 4%

profile of v6, /device:TPU:6, one launch (start us, length us, event | category | flops | bytes accessed | tf_op | source)
XLA Modules:
  0.0 49.2 jit_solution(5064523688354066647)
XLA Ops:
  0.6 0.9 %shard_map.93 = (f32[64,1,768]{2,1,0:T(1,128)S(1)}, bf16[64,256]{1,0:T(8,128)(2,1)S(1)}, bf16[64,256]{1,0:T(8,128)(2,1)S(1)}, bf16[64,256]{1,0:T(8,128)(2,1)S(1)}) custom-call(bf16[64,256]{1,0:T(8,128)(2,1)} %key_far.1, bf16[64,256]{1,0:T(8,128)(2,1)} %value_far.1, bf16[64,256]{1,0:T(8,128)(2,1)} %grad_far.1, bf16[64,256]{1,0:T(8,128)(2,1)} %query_far.1, ...), custom_call_target="tpu_custom_call" | custom-call | tf_op jit(solution)/shard_map/pallas_call | solution.py:191
  1.5 22.0 %all_to_all.10.own_ref.refs_1_ = f32[64,1,768]{2,1,0:T(1,128)S(1)} all-to-all(f32[64,1,768]{2,1,0:T(1,128)S(1)} %get-tuple-element.11), channel_id=1, replica_groups={{200,72,204,76,192,64,196,68,248,120,252,124,240,112,244,116,168,40,172..., dimensions={0} | all-to-all | bytes 393216 | tf_op jit(solution)/shard_map/all_to_all | solution.py:213
  23.6 0.0 collective-permute-start
  23.6 1.4 %shard_map.94.refs_3_ = bf16[11,256,256]{2,1,0:T(8,128)(2,1)S(1)} custom-call(f32[64,1,768]{2,1,0:T(1,128)S(1)} %all_to_all.10.own_ref.refs_1_, bf16[11,256,256]{2,1,0:T(8,128)(2,1)} %constant.21.clone.bank_far), custom_call_target="tpu_custom_call" | custom-call | tf_op jit(solution)/shard_map/pallas_call | solution.py:191
  24.9 0.1 collective-permute-done.refs_2_
  25.0 1.5 %shard_map.95 = f32[64,1,768]{2,1,0:T(1,128)S(1)} custom-call(s32[1]{0:T(128)} %bitcast.refs_0_, f32[64,1,768]{2,1,0:T(1,128)S(1)} %all_to_all.10.own_ref.refs_1_, f32[64,1,768]{2,1,0:T(1,128)S(1)} %collective-permute-done.refs_2_, bf16[11,256,256]{2,1,0:T(8,128)(2,1)S(1)} %shard_map.94.refs_3_), custom_call_target="tpu_custom_call" | custom-call | tf_op jit(solution)/shard_map/pallas_call | solution.py:191
  26.5 18.4 %all_to_all.11.moved_ref = f32[64,1,768]{2,1,0:T(1,128)S(1)} all-to-all(f32[64,1,768]{2,1,0:T(1,128)S(1)} %shard_map.95), channel_id=1, replica_groups={{200,72,204,76,192,64,196,68,248,120,252,124,240,112,244,116,168,40,172..., dimensions={0} | all-to-all | bytes 393216 | tf_op jit(solution)/shard_map/all_to_all | solution.py:213
  44.9 0.1 collective-permute-start.1
  45.0 0.7 %shard_map.96 = (bf16[64,256]{1,0:T(8,128)(2,1)}, bf16[64,256]{1,0:T(8,128)(2,1)}, bf16[64,256]{1,0:T(8,128)(2,1)}) custom-call(f32[64,1,768]{2,1,0:T(1,128)S(1)} %all_to_all.11.moved_ref, bf16[64,256]{1,0:T(8,128)(2,1)S(1)} %get-tuple-element.12.key_ref, bf16[64,256]{1,0:T(8,128)(2,1)S(1)} %get-tuple-element.13.value_ref, ...), custom_call_target="tpu_custom_call" | custom-call | tf_op jit(solution)/shard_map/pallas_call | solution.py:191
  45.7 2.9 %collective-permute-done.1.right_ref = f32[1,256]{1,0:T(1,128)S(1)} collective-permute-done((f32[1,256]{1,0:T(1,128)S(1)}, f32[1,256]{1,0:T(1,128)S(1)}, u32[]{:S(2)}, u32[]{:S(2)}) %collective-permute-start.1) | collective-permute-done | bytes 1056 | tf_op jit(solution)/shard_map/ppermute | solution.py:248
  48.6 0.6 %shard_map.98 = f32[1,256]{1,0:T(1,128)} custom-call(f32[1,256]{1,0:T(1,128)S(1)} %shard_map.97.left_ref, f32[1,256]{1,0:T(1,128)S(1)} %collective-permute-done.1.right_ref), custom_call_target="tpu_custom_call" | custom-call | tf_op jit(solution)/shard_map/pallas_call | solution.py:191
  (1 shorter events, 0.0 us)
Async XLA Ops:
  23.6 1.4 %collective-permute-start = (f32[64,1,768]{2,1,0:T(1,128)S(1)}, f32[64,1,768]{2,1,0:T(1,128)S(1)}, u32[]{:S(2)}, u32[]{:S(2)}) collective-permute-start(f32[64,1,768]{2,1,0:T(1,128)S(1)} %all_to_all.10.own_ref.refs_1_), channel_id=1, source_target_pairs={{0,2},{2,0},{4,6},{6,4},{8,10},{10,8},{12,14},{14,12},{16,18},{18,... | collective-permute-start | bytes 589832 | tf_op jit(solution)/shard_map/ppermute | solution.py:235
  44.9 3.7 %collective-permute-start.1 = (f32[1,256]{1,0:T(1,128)S(1)}, f32[1,256]{1,0:T(1,128)S(1)}, u32[]{:S(2)}, u32[]{:S(2)}) collective-permute-start(f32[1,256]{1,0:T(1,128)S(1)} %shard_map.97.left_ref), channel_id=1, source_target_pairs={{0,1},{1,0},{2,3},{3,2},{4,5},{5,4},{6,7},{7,6},{8,9},{9,8},{10,11... | collective-permute-start | bytes 3080 | tf_op jit(solution)/shard_map/ppermute | solution.py:248

commit v7 on v6

--- a/solution.py
+++ b/solution.py
@@ -82,8 +82,10 @@
     out_ref[:, 0, 2 * width :] = jnp.broadcast_to(taps[...], key.shape)
 
 
-def lead_body(own_ref, bank_far, bank_ref, arrived):
-    for copy in fetch([(bank_far, bank_ref)], arrived):
+def lead_body(parity_ref, own_ref, bank_far, bank_ref, arrived):
+    spans = ((0, 0, AHEAD), (AHEAD + 2 * parity_ref[0], AHEAD, 2), (BACK, AHEAD + 2, 3))
+    pairs = [(bank_far.at[pl.ds(first, count)], bank_ref.at[pl.ds(place, count)]) for first, place, count in spans]
+    for copy in fetch(pairs, arrived):
         copy.wait()
 
 
@@ -92,14 +94,14 @@
     width = bank_ref.shape[2]
     half = width // 2
     rows = 2 * own_ref.shape[0]
-    ahead = bank_ref[pl.ds(AHEAD + 2 * parity, 2)].reshape(2 * width, width)
+    ahead = bank_ref[AHEAD : AHEAD + 2].reshape(2 * width, width)
     signal = jnp.concatenate([own_ref[:, 0, :], other_ref[:, 0, :]], axis=0)
     data = jnp.concatenate(split(signal), axis=0)
     fronts = []
     for index in range(3):
         wide = product(ahead, data[:, index * width : (index + 1) * width])
         fronts.append(wide[: 2 * rows] + wide[2 * rows :])
-    twist = [bank_ref[TWIST + i].astype(jnp.float32) for i in (0, 1)]
+    twist = [bank_ref[AHEAD + 3 + i].astype(jnp.float32) for i in (0, 1)]
     cosine, sine = [table[:rows] + table[rows:] for table in twist]
     reals = [[] for _ in range(3)]
     imags = [[] for _ in range(3)]
@@ -161,7 +163,7 @@
         outs[key] = inner_product(mixes[key], bank_ref, key[1], True)
     for part in range(PARTS):
         untwist(part)
-    table = bank_ref[BACK, pl.ds(pl.multiple_of(rows * parity, rows), rows)]
+    table = bank_ref[AHEAD + 2, pl.ds(pl.multiple_of(rows * parity, rows), rows)]
     for index in range(3):
         high, low = split(jnp.concatenate(reals[index] + imags[index], axis=0))
         wide = product(table, high)
@@ -235,11 +237,11 @@
     other = lax.ppermute(own, "ctx", other_core)
     near_bank = kernel_call(
         lead_body,
-        jax.ShapeDtypeStruct(bank.shape, bank.dtype),
+        jax.ShapeDtypeStruct((bank.shape[0] - 2,) + bank.shape[1:], bank.dtype),
         8,
-        (own, pltpu.with_memory_space_constraint(bank, pltpu.HBM)),
-        [near, far],
-        [pltpu.SemaphoreType.DMA((1,))],
+        (parity, own, pltpu.with_memory_space_constraint(bank, pltpu.HBM)),
+        [scalar, near, far],
+        [pltpu.SemaphoreType.DMA((3,))],
     )
     restored = kernel_call(middle, message, 24, (parity, own, other, near_bank), [scalar, near, near, near])
     moved = exchange(restored)

time: 49.4 us -> 49.3 us (level)
  no operation moved by 1% of the time
where the time goes in v7:
time: 49.3 us; the launch traced here: 49.1 us
  blocking collectives  40.3 us (82%)
  Pallas kernels  4.97 us (10%)
  waiting for transfers between devices  3.05 us (6%)
  between operations  0.67 us (1%)
    all_to_all x2, blocking collectives, exchange(): lax.all_to_all(array, 'ctx', 0, 0, axis_index_groups=same_core, tiled=True)  40.3 us
    pallas_call x6, Pallas kernels, kernel_call(): pl.pallas_call(body, out_shape=out_shape, in_specs=in_specs, scratch_shap...  4.97 us
    ppermute x1, waiting for transfers between devices, shards(): swapped = lax.ppermute(partial, 'ch', [(0, 1), (1, 0)])  2.87 us
  transfers between devices with their start and end apart: 2, of which 2 were waited for; matrix products, arithmetic and copies ran while one was open for 0% of the time, Pallas kernels for 4%

profile of v7, /device:TPU:6, one launch (start us, length us, event | category | flops | bytes accessed | tf_op | source)
XLA Modules:
  0.0 49.1 jit_solution(3659363748079463122)
XLA Ops:
  0.6 0.9 %shard_map.93 = (f32[64,1,768]{2,1,0:T(1,128)S(1)}, bf16[64,256]{1,0:T(8,128)(2,1)S(1)}, bf16[64,256]{1,0:T(8,128)(2,1)S(1)}, bf16[64,256]{1,0:T(8,128)(2,1)S(1)}) custom-call(bf16[64,256]{1,0:T(8,128)(2,1)} %key_far.1, bf16[64,256]{1,0:T(8,128)(2,1)} %value_far.1, bf16[64,256]{1,0:T(8,128)(2,1)} %grad_far.1, bf16[64,256]{1,0:T(8,128)(2,1)} %query_far.1, ...), custom_call_target="tpu_custom_call" | custom-call | tf_op jit(solution)/shard_map/pallas_call | solution.py:193
  1.5 22.0 %all_to_all.10.own_ref.refs_1_ = f32[64,1,768]{2,1,0:T(1,128)S(1)} all-to-all(f32[64,1,768]{2,1,0:T(1,128)S(1)} %get-tuple-element.11), channel_id=1, replica_groups={{200,72,204,76,192,64,196,68,248,120,252,124,240,112,244,116,168,40,172..., dimensions={0} | all-to-all | bytes 393216 | tf_op jit(solution)/shard_map/all_to_all | solution.py:215
  23.6 0.0 collective-permute-start
  23.6 1.3 %shard_map.94.refs_3_ = bf16[9,256,256]{2,1,0:T(8,128)(2,1)S(1)} custom-call(s32[1]{0:T(128)} %bitcast.parity_ref.refs_0_, f32[64,1,768]{2,1,0:T(1,128)S(1)} %all_to_all.10.own_ref.refs_1_, bf16[11,256,256]{2,1,0:T(8,128)(2,1)} %constant.21.clone.bank_far), custom_call_target="tpu_custom_call" | custom-call | tf_op jit(solution)/shard_map/pallas_call | solution.py:193
  24.8 0.2 collective-permute-done.refs_2_
  25.0 1.5 %shard_map.95 = f32[64,1,768]{2,1,0:T(1,128)S(1)} custom-call(s32[1]{0:T(128)} %bitcast.parity_ref.refs_0_, f32[64,1,768]{2,1,0:T(1,128)S(1)} %all_to_all.10.own_ref.refs_1_, f32[64,1,768]{2,1,0:T(1,128)S(1)} %collective-permute-done.refs_2_, bf16[9,256,256]{2,1,0:T(8,128)(2,1)S(1)} %shard_map.94.refs_3_), custom_call_target="tpu_custom_call" | custom-call | tf_op jit(solution)/shard_map/pallas_call | solution.py:193
  26.5 18.3 %all_to_all.11.moved_ref = f32[64,1,768]{2,1,0:T(1,128)S(1)} all-to-all(f32[64,1,768]{2,1,0:T(1,128)S(1)} %shard_map.95), channel_id=1, replica_groups={{200,72,204,76,192,64,196,68,248,120,252,124,240,112,244,116,168,40,172..., dimensions={0} | all-to-all | bytes 393216 | tf_op jit(solution)/shard_map/all_to_all | solution.py:215
  44.8 0.1 collective-permute-start.1
  44.9 0.7 %shard_map.96 = (bf16[64,256]{1,0:T(8,128)(2,1)}, bf16[64,256]{1,0:T(8,128)(2,1)}, bf16[64,256]{1,0:T(8,128)(2,1)}) custom-call(f32[64,1,768]{2,1,0:T(1,128)S(1)} %all_to_all.11.moved_ref, bf16[64,256]{1,0:T(8,128)(2,1)S(1)} %get-tuple-element.12.key_ref, bf16[64,256]{1,0:T(8,128)(2,1)S(1)} %get-tuple-element.13.value_ref, ...), custom_call_target="tpu_custom_call" | custom-call | tf_op jit(solution)/shard_map/pallas_call | solution.py:193
  45.6 2.9 %collective-permute-done.1.right_ref = f32[1,256]{1,0:T(1,128)S(1)} collective-permute-done((f32[1,256]{1,0:T(1,128)S(1)}, f32[1,256]{1,0:T(1,128)S(1)}, u32[]{:S(2)}, u32[]{:S(2)}) %collective-permute-start.1) | collective-permute-done | bytes 1056 | tf_op jit(solution)/shard_map/ppermute | solution.py:250
  48.5 0.6 %shard_map.98 = f32[1,256]{1,0:T(1,128)} custom-call(f32[1,256]{1,0:T(1,128)S(1)} %shard_map.97.left_ref, f32[1,256]{1,0:T(1,128)S(1)} %collective-permute-done.1.right_ref), custom_call_target="tpu_custom_call" | custom-call | tf_op jit(solution)/shard_map/pallas_call | solution.py:193
  (1 shorter events, 0.0 us)
Async XLA Ops:
  23.6 1.4 %collective-permute-start = (f32[64,1,768]{2,1,0:T(1,128)S(1)}, f32[64,1,768]{2,1,0:T(1,128)S(1)}, u32[]{:S(2)}, u32[]{:S(2)}) collective-permute-start(f32[64,1,768]{2,1,0:T(1,128)S(1)} %all_to_all.10.own_ref.refs_1_), channel_id=1, source_target_pairs={{0,2},{2,0},{4,6},{6,4},{8,10},{10,8},{12,14},{14,12},{16,18},{18,... | collective-permute-start | bytes 589832 | tf_op jit(solution)/shard_map/ppermute | solution.py:237
  44.8 3.7 %collective-permute-start.1 = (f32[1,256]{1,0:T(1,128)S(1)}, f32[1,256]{1,0:T(1,128)S(1)}, u32[]{:S(2)}, u32[]{:S(2)}) collective-permute-start(f32[1,256]{1,0:T(1,128)S(1)} %shard_map.97.left_ref), channel_id=1, source_target_pairs={{0,1},{1,0},{2,3},{3,2},{4,5},{5,4},{6,7},{7,6},{8,9},{9,8},{10,11... | collective-permute-start | bytes 3080 | tf_op jit(solution)/shard_map/ppermute | solution.py:250

commit v8 on v7

--- a/solution.py
+++ b/solution.py
@@ -12,7 +12,7 @@
 MIB = 1024 * 1024
 PARTS = 2
 ORDER = np.array([((1 - x) * 8 + (4 + 3 * z) % 8) * 4 + (2 + y) % 4 for z in range(8) for y in range(4) for x in range(2)])
-AHEAD, BACK, TWIST = 4, 8, 9
+AHEAD, BACK, TWIST = 4, 6, 7
 
 
 def halves(values):
@@ -34,8 +34,7 @@
     block_table = np.concatenate([np.cos(block_angle), -np.sin(block_angle)], axis=0)
     own = [2 * ORDER + parity for parity in (0, 1)]
     for e in (0, 1):
-        high, low = halves(np.concatenate([block_table[:, own[e]], block_table[:, own[1 - e]]], axis=1))
-        planes += [np.concatenate([high, high], axis=1), np.concatenate([low, np.zeros_like(low)], axis=1)]
+        planes.append(np.concatenate(halves(block_table[:, own[e]]) * 2, axis=1))
     pieces = [np.concatenate(halves(block_table.T[own[e]] / length), axis=0) for e in (0, 1)]
     planes.append(np.concatenate(pieces, axis=0))
     twist_angle = 2.0 * math.pi * np.outer(rows, np.arange(width)) / length
@@ -82,26 +81,32 @@
     out_ref[:, 0, 2 * width :] = jnp.broadcast_to(taps[...], key.shape)
 
 
-def lead_body(parity_ref, own_ref, bank_far, bank_ref, arrived):
-    spans = ((0, 0, AHEAD), (AHEAD + 2 * parity_ref[0], AHEAD, 2), (BACK, AHEAD + 2, 3))
-    pairs = [(bank_far.at[pl.ds(first, count)], bank_ref.at[pl.ds(place, count)]) for first, place, count in spans]
-    for copy in fetch(pairs, arrived):
-        copy.wait()
-
-
-def middle_body(scale, parity_ref, own_ref, other_ref, bank_ref, out_ref):
+def front_products(blocks_ref, table):
+    width = table.shape[1]
+    twice = jnp.concatenate([blocks_ref[:, 0, :], blocks_ref[:, 0, :]], axis=0)
+    data = jnp.concatenate(split(twice), axis=0)
+    return [product(table, data[:, index * width : (index + 1) * width]) for index in range(3)]
+
+
+def lead_body(parity_ref, own_ref, bank_far, bank_ref, front_ref, arrived):
+    spans = ((AHEAD, 2), (0, AHEAD), (BACK, 3))
+    pairs = [(bank_far.at[pl.ds(first, count)], bank_ref.at[pl.ds(first, count)]) for first, count in spans]
+    copies = fetch(pairs, arrived)
+    copies[0].wait()
+    for index, front in enumerate(front_products(own_ref, bank_ref[AHEAD + parity_ref[0]])):
+        front_ref[index] = front
+    copies[1].wait()
+    copies[2].wait()
+
+
+def middle_body(scale, parity_ref, other_ref, front_ref, bank_ref, out_ref):
     parity = parity_ref[0]
     width = bank_ref.shape[2]
     half = width // 2
-    rows = 2 * own_ref.shape[0]
-    ahead = bank_ref[AHEAD : AHEAD + 2].reshape(2 * width, width)
-    signal = jnp.concatenate([own_ref[:, 0, :], other_ref[:, 0, :]], axis=0)
-    data = jnp.concatenate(split(signal), axis=0)
-    fronts = []
-    for index in range(3):
-        wide = product(ahead, data[:, index * width : (index + 1) * width])
-        fronts.append(wide[: 2 * rows] + wide[2 * rows :])
-    twist = [bank_ref[AHEAD + 3 + i].astype(jnp.float32) for i in (0, 1)]
+    rows = 2 * other_ref.shape[0]
+    others = front_products(other_ref, bank_ref[AHEAD + 1 - parity])
+    fronts = [front_ref[index] + others[index] for index in range(3)]
+    twist = [bank_ref[TWIST + i].astype(jnp.float32) for i in (0, 1)]
     cosine, sine = [table[:rows] + table[rows:] for table in twist]
     reals = [[] for _ in range(3)]
     imags = [[] for _ in range(3)]
@@ -163,7 +168,7 @@
         outs[key] = inner_product(mixes[key], bank_ref, key[1], True)
     for part in range(PARTS):
         untwist(part)
-    table = bank_ref[AHEAD + 2, pl.ds(pl.multiple_of(rows * parity, rows), rows)]
+    table = bank_ref[BACK, pl.ds(pl.multiple_of(rows * parity, rows), rows)]
     for index in range(3):
         high, low = split(jnp.concatenate(reals[index] + imags[index], axis=0))
         wide = product(table, high)
@@ -235,15 +240,18 @@
     )
     own = exchange(packed)
     other = lax.ppermute(own, "ctx", other_core)
-    near_bank = kernel_call(
+    near_bank, front = kernel_call(
         lead_body,
-        jax.ShapeDtypeStruct((bank.shape[0] - 2,) + bank.shape[1:], bank.dtype),
+        (
+            jax.ShapeDtypeStruct(bank.shape, bank.dtype),
+            jax.ShapeDtypeStruct((3, 2 * devices, width), jnp.float32),
+        ),
         8,
         (parity, own, pltpu.with_memory_space_constraint(bank, pltpu.HBM)),
         [scalar, near, far],
         [pltpu.SemaphoreType.DMA((3,))],
     )
-    restored = kernel_call(middle, message, 24, (parity, own, other, near_bank), [scalar, near, near, near])
+    restored = kernel_call(middle, message, 24, (parity, other, front, near_bank), [scalar, near, near, near])
     moved = exchange(restored)
     line = jax.ShapeDtypeStruct((1, width), jnp.float32)
     partial = kernel_call(sum_body, line, 4, (moved,), [near])

time: 49.3 us -> 49.2 us (level)
  no operation moved by 1% of the time
where the time goes in v8:
time: 49.2 us; the launch traced here: 49 us
  blocking collectives  40.3 us (82%)
  Pallas kernels  4.9 us (10%)
  waiting for transfers between devices  3.04 us (6%)
  between operations  0.67 us (1%)
    all_to_all x2, blocking collectives, exchange(): lax.all_to_all(array, 'ctx', 0, 0, axis_index_groups=same_core, tiled=True)  40.3 us
    pallas_call x6, Pallas kernels, kernel_call(): pl.pallas_call(body, out_shape=out_shape, in_specs=in_specs, scratch_shap...  4.9 us
    ppermute x1, waiting for transfers between devices, shards(): swapped = lax.ppermute(partial, 'ch', [(0, 1), (1, 0)])  2.87 us
  transfers between devices with their start and end apart: 2, of which 2 were waited for; matrix products, arithmetic and copies ran while one was open for 0% of the time, Pallas kernels for 4%

profile of v8, /device:TPU:6, one launch (start us, length us, event | category | flops | bytes accessed | tf_op | source)
XLA Modules:
  0.0 49.0 jit_solution(12663058975384778654)
XLA Ops:
  0.6 0.9 %shard_map.93 = (f32[64,1,768]{2,1,0:T(1,128)S(1)}, bf16[64,256]{1,0:T(8,128)(2,1)S(1)}, bf16[64,256]{1,0:T(8,128)(2,1)S(1)}, bf16[64,256]{1,0:T(8,128)(2,1)S(1)}) custom-call(bf16[64,256]{1,0:T(8,128)(2,1)} %key_far.1, bf16[64,256]{1,0:T(8,128)(2,1)} %value_far.1, bf16[64,256]{1,0:T(8,128)(2,1)} %grad_far.1, bf16[64,256]{1,0:T(8,128)(2,1)} %query_far.1, ...), custom_call_target="tpu_custom_call" | custom-call | tf_op jit(solution)/shard_map/pallas_call | solution.py:198
  1.5 22.0 %all_to_all.10.own_ref = f32[64,1,768]{2,1,0:T(1,128)S(1)} all-to-all(f32[64,1,768]{2,1,0:T(1,128)S(1)} %get-tuple-element.13), channel_id=1, replica_groups={{200,72,204,76,192,64,196,68,248,120,252,124,240,112,244,116,168,40,172..., dimensions={0} | all-to-all | bytes 393216 | tf_op jit(solution)/shard_map/all_to_all | solution.py:220
  23.6 0.0 collective-permute-start
  23.6 1.3 %shard_map.94 = (bf16[9,256,256]{2,1,0:T(8,128)(2,1)S(1)}, f32[3,256,256]{2,1,0:T(8,128)S(1)}) custom-call(s32[1]{0:T(128)} %bitcast.parity_ref.refs_0_, f32[64,1,768]{2,1,0:T(1,128)S(1)} %all_to_all.10.own_ref, bf16[9,256,256]{2,1,0:T(8,128)(2,1)} %constant.21.clone.bank_far), custom_call_target="tpu_custom_call" | custom-call | tf_op jit(solution)/shard_map/pallas_call | solution.py:198
  24.8 0.2 collective-permute-done.refs_1_
  25.0 1.5 %shard_map.95 = f32[64,1,768]{2,1,0:T(1,128)S(1)} custom-call(s32[1]{0:T(128)} %bitcast.parity_ref.refs_0_, f32[64,1,768]{2,1,0:T(1,128)S(1)} %collective-permute-done.refs_1_, f32[3,256,256]{2,1,0:T(8,128)S(1)} %get-tuple-element.14.refs_2_, bf16[9,256,256]{2,1,0:T(8,128)(2,1)S(1)} %get-tuple-element.15.refs_3_), custom_call_target="tpu_custom_call" | custom-call | tf_op jit(solution)/shard_map/pallas_call | solution.py:198
  26.5 18.3 %all_to_all.11.moved_ref = f32[64,1,768]{2,1,0:T(1,128)S(1)} all-to-all(f32[64,1,768]{2,1,0:T(1,128)S(1)} %shard_map.95), channel_id=1, replica_groups={{200,72,204,76,192,64,196,68,248,120,252,124,240,112,244,116,168,40,172..., dimensions={0} | all-to-all | bytes 393216 | tf_op jit(solution)/shard_map/all_to_all | solution.py:220
  44.8 0.1 collective-permute-start.1
  44.9 0.7 %shard_map.96 = (bf16[64,256]{1,0:T(8,128)(2,1)}, bf16[64,256]{1,0:T(8,128)(2,1)}, bf16[64,256]{1,0:T(8,128)(2,1)}) custom-call(f32[64,1,768]{2,1,0:T(1,128)S(1)} %all_to_all.11.moved_ref, bf16[64,256]{1,0:T(8,128)(2,1)S(1)} %get-tuple-element.16.key_ref, bf16[64,256]{1,0:T(8,128)(2,1)S(1)} %get-tuple-element.17.value_ref, ...), custom_call_target="tpu_custom_call" | custom-call | tf_op jit(solution)/shard_map/pallas_call | solution.py:198
  45.6 2.9 %collective-permute-done.1.right_ref = f32[1,256]{1,0:T(1,128)S(1)} collective-permute-done((f32[1,256]{1,0:T(1,128)S(1)}, f32[1,256]{1,0:T(1,128)S(1)}, u32[]{:S(2)}, u32[]{:S(2)}) %collective-permute-start.1) | collective-permute-done | bytes 1056 | tf_op jit(solution)/shard_map/ppermute | solution.py:258
  48.4 0.6 %shard_map.98 = f32[1,256]{1,0:T(1,128)} custom-call(f32[1,256]{1,0:T(1,128)S(1)} %shard_map.97.left_ref, f32[1,256]{1,0:T(1,128)S(1)} %collective-permute-done.1.right_ref), custom_call_target="tpu_custom_call" | custom-call | tf_op jit(solution)/shard_map/pallas_call | solution.py:198
  (1 shorter events, 0.0 us)
Async XLA Ops:
  23.6 1.4 %collective-permute-start = (f32[64,1,768]{2,1,0:T(1,128)S(1)}, f32[64,1,768]{2,1,0:T(1,128)S(1)}, u32[]{:S(2)}, u32[]{:S(2)}) collective-permute-start(f32[64,1,768]{2,1,0:T(1,128)S(1)} %all_to_all.10.own_ref), channel_id=1, source_target_pairs={{0,2},{2,0},{4,6},{6,4},{8,10},{10,8},{12,14},{14,12},{16,18},{18,... | collective-permute-start | bytes 589832 | tf_op jit(solution)/shard_map/ppermute | solution.py:242
  44.8 3.7 %collective-permute-start.1 = (f32[1,256]{1,0:T(1,128)S(1)}, f32[1,256]{1,0:T(1,128)S(1)}, u32[]{:S(2)}, u32[]{:S(2)}) collective-permute-start(f32[1,256]{1,0:T(1,128)S(1)} %shard_map.97.left_ref), channel_id=1, source_target_pairs={{0,1},{1,0},{2,3},{3,2},{4,5},{5,4},{6,7},{7,6},{8,9},{9,8},{10,11... | collective-permute-start | bytes 3080 | tf_op jit(solution)/shard_map/ppermute | solution.py:258

commit v9 on v8

--- a/solution.py
+++ b/solution.py
@@ -182,16 +182,13 @@
     out_ref[...] = jnp.sum(moved_ref[:, 0, 2 * width :], axis=0, keepdims=True)
 
 
-def finish_body(moved_ref, key_ref, value_ref, grad_ref, query_out, key_out, value_out):
+def finish_body(moved_ref, key_ref, value_ref, grad_ref, left_ref, right_ref, query_out, key_out, value_out, filter_out):
     width = key_ref.shape[1]
+    filter_out[...] = left_ref[...] + right_ref[...]
     back = moved_ref[:, 0, width : 2 * width]
     query_out[...] = (grad_ref[...].astype(jnp.float32) * moved_ref[:, 0, :width]).astype(jnp.bfloat16)
     key_out[...] = (back * value_ref[...].astype(jnp.float32)).astype(jnp.bfloat16)
     value_out[...] = (back * key_ref[...].astype(jnp.float32)).astype(jnp.bfloat16)
-
-
-def add_body(left_ref, right_ref, out_ref):
-    out_ref[...] = left_ref[...] + right_ref[...]
 
 
 def kernel_call(body, out_shape, limit, operands, in_specs, scratch=()):
@@ -256,10 +253,10 @@
     line = jax.ShapeDtypeStruct((1, width), jnp.float32)
     partial = kernel_call(sum_body, line, 4, (moved,), [near])
     swapped = lax.ppermute(partial, "ch", [(0, 1), (1, 0)])
-    query_grad, key_grad, value_grad = kernel_call(
-        finish_body, (narrow, narrow, narrow), 4, (moved, key, value, grad), [near] * 4
-    )
-    filter_grad = kernel_call(add_body, line, 4, (partial, swapped), [near, near]).reshape(width)
+    query_grad, key_grad, value_grad, filter_grad = kernel_call(
+        finish_body, (narrow, narrow, narrow, line), 4, (moved, key, value, grad, partial, swapped), [near] * 6
+    )
+    filter_grad = filter_grad.reshape(width)
     return (query_grad, key_grad, value_grad, filter_grad)
 
 

time: 49.2 us -> 49.4 us (level)
  waiting for transfers between devices: 3.04 us -> 3.72 us
  Pallas kernels: 4.9 us -> 4.34 us
    ppermute x1, waiting for transfers between devices: 2.87 us -> 3.56 us  [shards(): swapped = lax.ppermute(partial, 'ch', [(0, 1), (1, 0)])]
    pallas_call x6 -> x5, Pallas kernels: 4.9 us -> 4.34 us  [kernel_call(): pl.pallas_call(body, out_shape=out_shape, in_specs=in_specs, scratch_shap...]
  transfers between devices with their start and end apart: 2 -> 2, of which waited for: 2 -> 2; matrix products, arithmetic and copies ran while one was open for 0% -> 0% of each run, Pallas kernels for 4% -> 3%
where the time goes in v9:
time: 49.4 us; the launch traced here: 49.1 us
  blocking collectives  40.3 us (82%)
  Pallas kernels  4.34 us (9%)
  waiting for transfers between devices  3.72 us (8%)
  between operations  0.67 us (1%)
    all_to_all x2, blocking collectives, exchange(): lax.all_to_all(array, 'ctx', 0, 0, axis_index_groups=same_core, tiled=True)  40.3 us
    pallas_call x5, Pallas kernels, kernel_call(): pl.pallas_call(body, out_shape=out_shape, in_specs=in_specs, scratch_shap...  4.34 us
    ppermute x1, waiting for transfers between devices, shards(): swapped = lax.ppermute(partial, 'ch', [(0, 1), (1, 0)])  3.56 us
  transfers between devices with their start and end apart: 2, of which 2 were waited for; matrix products, arithmetic and copies ran while one was open for 0% of the time, Pallas kernels for 3%

profile of v9, /device:TPU:6, one launch (start us, length us, event | category | flops | bytes accessed | tf_op | source)
XLA Modules:
  0.0 49.1 jit_solution(15399378582911734729)
XLA Ops:
  0.6 0.9 %shard_map.93 = (f32[64,1,768]{2,1,0:T(1,128)S(1)}, bf16[64,256]{1,0:T(8,128)(2,1)S(1)}, bf16[64,256]{1,0:T(8,128)(2,1)S(1)}, bf16[64,256]{1,0:T(8,128)(2,1)S(1)}) custom-call(bf16[64,256]{1,0:T(8,128)(2,1)} %key_far.1, bf16[64,256]{1,0:T(8,128)(2,1)} %value_far.1, bf16[64,256]{1,0:T(8,128)(2,1)} %grad_far.1, bf16[64,256]{1,0:T(8,128)(2,1)} %query_far.1, ...), custom_call_target="tpu_custom_call" | custom-call | tf_op jit(solution)/shard_map/pallas_call | solution.py:195
  1.5 22.0 %all_to_all.10.own_ref = f32[64,1,768]{2,1,0:T(1,128)S(1)} all-to-all(f32[64,1,768]{2,1,0:T(1,128)S(1)} %get-tuple-element.14), channel_id=1, replica_groups={{200,72,204,76,192,64,196,68,248,120,252,124,240,112,244,116,168,40,172..., dimensions={0} | all-to-all | bytes 393216 | tf_op jit(solution)/shard_map/all_to_all | solution.py:217
  23.6 0.0 collective-permute-start
  23.6 1.3 %shard_map.94 = (bf16[9,256,256]{2,1,0:T(8,128)(2,1)S(1)}, f32[3,256,256]{2,1,0:T(8,128)S(1)}) custom-call(s32[1]{0:T(128)} %bitcast.parity_ref.refs_0_, f32[64,1,768]{2,1,0:T(1,128)S(1)} %all_to_all.10.own_ref, bf16[9,256,256]{2,1,0:T(8,128)(2,1)} %constant.21.clone.bank_far), custom_call_target="tpu_custom_call" | custom-call | tf_op jit(solution)/shard_map/pallas_call | solution.py:195
  24.8 0.2 collective-permute-done.refs_1_
  25.0 1.5 %shard_map.95 = f32[64,1,768]{2,1,0:T(1,128)S(1)} custom-call(s32[1]{0:T(128)} %bitcast.parity_ref.refs_0_, f32[64,1,768]{2,1,0:T(1,128)S(1)} %collective-permute-done.refs_1_, f32[3,256,256]{2,1,0:T(8,128)S(1)} %get-tuple-element.15.refs_2_, bf16[9,256,256]{2,1,0:T(8,128)(2,1)S(1)} %get-tuple-element.16.refs_3_), custom_call_target="tpu_custom_call" | custom-call | tf_op jit(solution)/shard_map/pallas_call | solution.py:195
  26.5 18.3 %all_to_all.11.moved_ref = f32[64,1,768]{2,1,0:T(1,128)S(1)} all-to-all(f32[64,1,768]{2,1,0:T(1,128)S(1)} %shard_map.95), channel_id=1, replica_groups={{200,72,204,76,192,64,196,68,248,120,252,124,240,112,244,116,168,40,172..., dimensions={0} | all-to-all | bytes 393216 | tf_op jit(solution)/shard_map/all_to_all | solution.py:217
  44.8 0.1 collective-permute-start.1
  44.9 3.6 %collective-permute-done.1.right_ref = f32[1,256]{1,0:T(1,128)S(1)} collective-permute-done((f32[1,256]{1,0:T(1,128)S(1)}, f32[1,256]{1,0:T(1,128)S(1)}, u32[]{:S(2)}, u32[]{:S(2)}) %collective-permute-start.1) | collective-permute-done | bytes 1056 | tf_op jit(solution)/shard_map/ppermute | solution.py:255
  48.4 0.7 %shard_map.97 = (bf16[64,256]{1,0:T(8,128)(2,1)}, bf16[64,256]{1,0:T(8,128)(2,1)}, bf16[64,256]{1,0:T(8,128)(2,1)}, f32[1,256]{1,0:T(1,128)}) custom-call(f32[64,1,768]{2,1,0:T(1,128)S(1)} %all_to_all.11.moved_ref, bf16[64,256]{1,0:T(8,128)(2,1)S(1)} %get-tuple-element.17.key_ref, bf16[64,256]{1,0:T(8,128)(2,1)S(1)} %get-tuple-element.18.value_ref, ...), custom_call_target="tpu_custom_call" | custom-call | tf_op jit(solution)/shard_map/pallas_call | solution.py:195
  (1 shorter events, 0.0 us)
Async XLA Ops:
  23.6 1.4 %collective-permute-start = (f32[64,1,768]{2,1,0:T(1,128)S(1)}, f32[64,1,768]{2,1,0:T(1,128)S(1)}, u32[]{:S(2)}, u32[]{:S(2)}) collective-permute-start(f32[64,1,768]{2,1,0:T(1,128)S(1)} %all_to_all.10.own_ref), channel_id=1, source_target_pairs={{0,2},{2,0},{4,6},{6,4},{8,10},{10,8},{12,14},{14,12},{16,18},{18,... | collective-permute-start | bytes 589832 | tf_op jit(solution)/shard_map/ppermute | solution.py:239
  44.8 3.7 %collective-permute-start.1 = (f32[1,256]{1,0:T(1,128)S(1)}, f32[1,256]{1,0:T(1,128)S(1)}, u32[]{:S(2)}, u32[]{:S(2)}) collective-permute-start(f32[1,256]{1,0:T(1,128)S(1)} %shard_map.96.left_ref), channel_id=1, source_target_pairs={{0,1},{1,0},{2,3},{3,2},{4,5},{5,4},{6,7},{7,6},{8,9},{9,8},{10,11... | collective-permute-start | bytes 3080 | tf_op jit(solution)/shard_map/ppermute | solution.py:255

commit v10 on v8

--- a/solution.py
+++ b/solution.py
@@ -88,26 +88,29 @@
     return [product(table, data[:, index * width : (index + 1) * width]) for index in range(3)]
 
 
-def lead_body(parity_ref, own_ref, bank_far, bank_ref, front_ref, arrived):
+def lead_body(parity_ref, own_ref, bank_far, bank_ref, front_ref, twist_ref, arrived):
     spans = ((AHEAD, 2), (0, AHEAD), (BACK, 3))
     pairs = [(bank_far.at[pl.ds(first, count)], bank_ref.at[pl.ds(first, count)]) for first, count in spans]
     copies = fetch(pairs, arrived)
     copies[0].wait()
     for index, front in enumerate(front_products(own_ref, bank_ref[AHEAD + parity_ref[0]])):
         front_ref[index] = front
+    copies[2].wait()
+    rows = twist_ref.shape[1]
+    for index in (0, 1):
+        table = bank_ref[TWIST + index].astype(jnp.float32)
+        twist_ref[index] = table[:rows] + table[rows:]
     copies[1].wait()
-    copies[2].wait()
-
-
-def middle_body(scale, parity_ref, other_ref, front_ref, bank_ref, out_ref):
+
+
+def middle_body(scale, parity_ref, other_ref, front_ref, twist_ref, bank_ref, out_ref):
     parity = parity_ref[0]
     width = bank_ref.shape[2]
     half = width // 2
     rows = 2 * other_ref.shape[0]
     others = front_products(other_ref, bank_ref[AHEAD + 1 - parity])
     fronts = [front_ref[index] + others[index] for index in range(3)]
-    twist = [bank_ref[TWIST + i].astype(jnp.float32) for i in (0, 1)]
-    cosine, sine = [table[:rows] + table[rows:] for table in twist]
+    cosine, sine = twist_ref[0], twist_ref[1]
     reals = [[] for _ in range(3)]
     imags = [[] for _ in range(3)]
     size = rows // PARTS
@@ -240,18 +243,19 @@
     )
     own = exchange(packed)
     other = lax.ppermute(own, "ctx", other_core)
-    near_bank, front = kernel_call(
+    near_bank, front, twist = kernel_call(
         lead_body,
         (
             jax.ShapeDtypeStruct(bank.shape, bank.dtype),
             jax.ShapeDtypeStruct((3, 2 * devices, width), jnp.float32),
+            jax.ShapeDtypeStruct((2, devices, width), jnp.float32),
         ),
         8,
         (parity, own, pltpu.with_memory_space_constraint(bank, pltpu.HBM)),
         [scalar, near, far],
         [pltpu.SemaphoreType.DMA((3,))],
     )
-    restored = kernel_call(middle, message, 24, (parity, other, front, near_bank), [scalar, near, near, near])
+    restored = kernel_call(middle, message, 24, (parity, other, front, twist, near_bank), [scalar] + [near] * 4)
     moved = exchange(restored)
     line = jax.ShapeDtypeStruct((1, width), jnp.float32)
     partial = kernel_call(sum_body, line, 4, (moved,), [near])

time: 49.2 us -> 49.3 us (level)
  no operation moved by 1% of the time
where the time goes in v10:
time: 49.3 us; the launch traced here: 49 us
  blocking collectives  40.3 us (82%)
  Pallas kernels  4.94 us (10%)
  waiting for transfers between devices  3.01 us (6%)
  between operations  0.67 us (1%)
    all_to_all x2, blocking collectives, exchange(): lax.all_to_all(array, 'ctx', 0, 0, axis_index_groups=same_core, tiled=True)  40.3 us
    pallas_call x6, Pallas kernels, kernel_call(): pl.pallas_call(body, out_shape=out_shape, in_specs=in_specs, scratch_shap...  4.94 us
    ppermute x1, waiting for transfers between devices, shards(): swapped = lax.ppermute(partial, 'ch', [(0, 1), (1, 0)])  2.87 us
  transfers between devices with their start and end apart: 2, of which 2 were waited for; matrix products, arithmetic and copies ran while one was open for 0% of the time, Pallas kernels for 4%

profile of v10, /device:TPU:6, one launch (start us, length us, event | category | flops | bytes accessed | tf_op | source)
XLA Modules:
  0.0 49.0 jit_solution(17521930712440149803)
XLA Ops:
  0.6 0.9 %shard_map.93 = (f32[64,1,768]{2,1,0:T(1,128)S(1)}, bf16[64,256]{1,0:T(8,128)(2,1)S(1)}, bf16[64,256]{1,0:T(8,128)(2,1)S(1)}, bf16[64,256]{1,0:T(8,128)(2,1)S(1)}) custom-call(bf16[64,256]{1,0:T(8,128)(2,1)} %key_far.1, bf16[64,256]{1,0:T(8,128)(2,1)} %value_far.1, bf16[64,256]{1,0:T(8,128)(2,1)} %grad_far.1, bf16[64,256]{1,0:T(8,128)(2,1)} %query_far.1, ...), custom_call_target="tpu_custom_call" | custom-call | tf_op jit(solution)/shard_map/pallas_call | solution.py:201
  1.5 22.0 %all_to_all.10.own_ref = f32[64,1,768]{2,1,0:T(1,128)S(1)} all-to-all(f32[64,1,768]{2,1,0:T(1,128)S(1)} %get-tuple-element.14), channel_id=1, replica_groups={{200,72,204,76,192,64,196,68,248,120,252,124,240,112,244,116,168,40,172..., dimensions={0} | all-to-all | bytes 393216 | tf_op jit(solution)/shard_map/all_to_all | solution.py:223
  23.6 0.0 collective-permute-start
  23.6 1.3 %shard_map.94 = (bf16[9,256,256]{2,1,0:T(8,128)(2,1)S(1)}, f32[3,256,256]{2,1,0:T(8,128)S(1)}, f32[2,128,256]{2,1,0:T(8,128)S(1)}) custom-call(s32[1]{0:T(128)} %bitcast.parity_ref.refs_0_, f32[64,1,768]{2,1,0:T(1,128)S(1)} %all_to_all.10.own_ref, bf16[9,256,256]{2,1,0:T(8,128)(2,1)} %constant.21.clone.bank_far), custom_call_target="tpu_custom_call" | custom-call | tf_op jit(solution)/shard_map/pallas_call | solution.py:201
  24.9 0.1 collective-permute-done.refs_1_
  25.0 1.5 %shard_map.95 = f32[64,1,768]{2,1,0:T(1,128)S(1)} custom-call(s32[1]{0:T(128)} %bitcast.parity_ref.refs_0_, f32[64,1,768]{2,1,0:T(1,128)S(1)} %collective-permute-done.refs_1_, f32[3,256,256]{2,1,0:T(8,128)S(1)} %get-tuple-element.15.refs_2_, f32[2,128,256]{2,1,0:T(8,128)S(1)} %get-tuple-element.16.refs_3_, bf16[9,256,256]{2,1,0:T(8,128)(2,1)S(1)} %get-tuple-element.17.refs_4_), custom_call_target="tpu_custom_call" | custom-call | tf_op jit(solution)/shard_map/pallas_call | solution.py:201
  26.5 18.3 %all_to_all.11.moved_ref = f32[64,1,768]{2,1,0:T(1,128)S(1)} all-to-all(f32[64,1,768]{2,1,0:T(1,128)S(1)} %shard_map.95), channel_id=1, replica_groups={{200,72,204,76,192,64,196,68,248,120,252,124,240,112,244,116,168,40,172..., dimensions={0} | all-to-all | bytes 393216 | tf_op jit(solution)/shard_map/all_to_all | solution.py:223
  44.8 0.1 collective-permute-start.1
  44.9 0.7 %shard_map.96 = (bf16[64,256]{1,0:T(8,128)(2,1)}, bf16[64,256]{1,0:T(8,128)(2,1)}, bf16[64,256]{1,0:T(8,128)(2,1)}) custom-call(f32[64,1,768]{2,1,0:T(1,128)S(1)} %all_to_all.11.moved_ref, bf16[64,256]{1,0:T(8,128)(2,1)S(1)} %get-tuple-element.18.key_ref, bf16[64,256]{1,0:T(8,128)(2,1)S(1)} %get-tuple-element.19.value_ref, ...), custom_call_target="tpu_custom_call" | custom-call | tf_op jit(solution)/shard_map/pallas_call | solution.py:201
  45.6 2.9 %collective-permute-done.1.right_ref = f32[1,256]{1,0:T(1,128)S(1)} collective-permute-done((f32[1,256]{1,0:T(1,128)S(1)}, f32[1,256]{1,0:T(1,128)S(1)}, u32[]{:S(2)}, u32[]{:S(2)}) %collective-permute-start.1) | collective-permute-done | bytes 1056 | tf_op jit(solution)/shard_map/ppermute | solution.py:262
  48.5 0.6 %shard_map.98 = f32[1,256]{1,0:T(1,128)} custom-call(f32[1,256]{1,0:T(1,128)S(1)} %shard_map.97.left_ref, f32[1,256]{1,0:T(1,128)S(1)} %collective-permute-done.1.right_ref), custom_call_target="tpu_custom_call" | custom-call | tf_op jit(solution)/shard_map/pallas_call | solution.py:201
  (1 shorter events, 0.0 us)
Async XLA Ops:
  23.6 1.4 %collective-permute-start = (f32[64,1,768]{2,1,0:T(1,128)S(1)}, f32[64,1,768]{2,1,0:T(1,128)S(1)}, u32[]{:S(2)}, u32[]{:S(2)}) collective-permute-start(f32[64,1,768]{2,1,0:T(1,128)S(1)} %all_to_all.10.own_ref), channel_id=1, source_target_pairs={{0,2},{2,0},{4,6},{6,4},{8,10},{10,8},{12,14},{14,12},{16,18},{18,... | collective-permute-start | bytes 589832 | tf_op jit(solution)/shard_map/ppermute | solution.py:245
  44.8 3.7 %collective-permute-start.1 = (f32[1,256]{1,0:T(1,128)S(1)}, f32[1,256]{1,0:T(1,128)S(1)}, u32[]{:S(2)}, u32[]{:S(2)}) collective-permute-start(f32[1,256]{1,0:T(1,128)S(1)} %shard_map.97.left_ref), channel_id=1, source_target_pairs={{0,1},{1,0},{2,3},{3,2},{4,5},{5,4},{6,7},{7,6},{8,9},{9,8},{10,11... | collective-permute-start | bytes 3080 | tf_op jit(solution)/shard_map/ppermute | solution.py:262

commit v11 on v10

--- a/solution.py
+++ b/solution.py
@@ -103,7 +103,7 @@
     copies[1].wait()
 
 
-def middle_body(scale, parity_ref, other_ref, front_ref, twist_ref, bank_ref, out_ref):
+def middle_body(parity_ref, other_ref, front_ref, twist_ref, bank_ref, out_ref):
     parity = parity_ref[0]
     width = bank_ref.shape[2]
     half = width // 2
@@ -139,8 +139,8 @@
         conv_imag = gated_real * taps_imag + gated_imag * taps_real
         back_real = grad_real * taps_real + grad_imag * taps_imag
         back_imag = grad_imag * taps_real - grad_real * taps_imag
-        cross_real = (grad_real * gated_real + grad_imag * gated_imag) * scale
-        cross_imag = (grad_imag * gated_real - grad_real * gated_imag) * scale
+        cross_real = grad_real * gated_real + grad_imag * gated_imag
+        cross_imag = grad_imag * gated_real - grad_real * gated_imag
         mixes[key] = jnp.concatenate(
             [
                 jnp.concatenate([conv_real, conv_imag], axis=1),
@@ -180,9 +180,9 @@
         )
 
 
-def sum_body(moved_ref, out_ref):
+def sum_body(scale, moved_ref, out_ref):
     width = out_ref.shape[1]
-    out_ref[...] = jnp.sum(moved_ref[:, 0, 2 * width :], axis=0, keepdims=True)
+    out_ref[...] = jnp.sum(moved_ref[:, 0, 2 * width :], axis=0, keepdims=True) * scale
 
 
 def finish_body(moved_ref, key_ref, value_ref, grad_ref, query_out, key_out, value_out):
@@ -222,8 +222,8 @@
     def exchange(array):
         return lax.all_to_all(array, "ctx", 0, 0, axis_index_groups=same_core, tiled=True)
 
-    def middle(*refs):
-        middle_body(scale, *refs)
+    def channel_sum(*refs):
+        sum_body(scale, *refs)
 
     far = pl.BlockSpec(memory_space=pltpu.HBM)
     key_far, value_far, grad_far, query_far, taps_far = [
@@ -255,10 +255,10 @@
         [scalar, near, far],
         [pltpu.SemaphoreType.DMA((3,))],
     )
-    restored = kernel_call(middle, message, 24, (parity, other, front, twist, near_bank), [scalar] + [near] * 4)
+    restored = kernel_call(middle_body, message, 24, (parity, other, front, twist, near_bank), [scalar] + [near] * 4)
     moved = exchange(restored)
     line = jax.ShapeDtypeStruct((1, width), jnp.float32)
-    partial = kernel_call(sum_body, line, 4, (moved,), [near])
+    partial = kernel_call(channel_sum, line, 4, (moved,), [near])
     swapped = lax.ppermute(partial, "ch", [(0, 1), (1, 0)])
     query_grad, key_grad, value_grad = kernel_call(
         finish_body, (narrow, narrow, narrow), 4, (moved, key, value, grad), [near] * 4

time: 49.3 us -> 49.3 us (level)
  no operation moved by 1% of the time
where the time goes in v11:
time: 49.3 us; the launch traced here: 49 us
  blocking collectives  40.3 us (82%)
  Pallas kernels  4.93 us (10%)
  waiting for transfers between devices  3.01 us (6%)
  between operations  0.67 us (1%)
    all_to_all x2, blocking collectives, exchange(): lax.all_to_all(array, 'ctx', 0, 0, axis_index_groups=same_core, tiled=True)  40.3 us
    pallas_call x6, Pallas kernels, kernel_call(): pl.pallas_call(body, out_shape=out_shape, in_specs=in_specs, scratch_shap...  4.93 us
    ppermute x1, waiting for transfers between devices, shards(): swapped = lax.ppermute(partial, 'ch', [(0, 1), (1, 0)])  2.87 us
  transfers between devices with their start and end apart: 2, of which 2 were waited for; matrix products, arithmetic and copies ran while one was open for 0% of the time, Pallas kernels for 4%

profile of v11, /device:TPU:6, one launch (start us, length us, event | category | flops | bytes accessed | tf_op | source)
XLA Modules:
  0.0 49.0 jit_solution(16011624240577336555)
XLA Ops:
  0.6 0.9 %shard_map.93 = (f32[64,1,768]{2,1,0:T(1,128)S(1)}, bf16[64,256]{1,0:T(8,128)(2,1)S(1)}, bf16[64,256]{1,0:T(8,128)(2,1)S(1)}, bf16[64,256]{1,0:T(8,128)(2,1)S(1)}) custom-call(bf16[64,256]{1,0:T(8,128)(2,1)} %key_far.1, bf16[64,256]{1,0:T(8,128)(2,1)} %value_far.1, bf16[64,256]{1,0:T(8,128)(2,1)} %grad_far.1, bf16[64,256]{1,0:T(8,128)(2,1)} %query_far.1, ...), custom_call_target="tpu_custom_call" | custom-call | tf_op jit(solution)/shard_map/pallas_call | solution.py:201
  1.5 22.0 %all_to_all.10.own_ref = f32[64,1,768]{2,1,0:T(1,128)S(1)} all-to-all(f32[64,1,768]{2,1,0:T(1,128)S(1)} %get-tuple-element.14), channel_id=1, replica_groups={{200,72,204,76,192,64,196,68,248,120,252,124,240,112,244,116,168,40,172..., dimensions={0} | all-to-all | bytes 393216 | tf_op jit(solution)/shard_map/all_to_all | solution.py:223
  23.6 0.0 collective-permute-start
  23.6 1.3 %shard_map.94 = (bf16[9,256,256]{2,1,0:T(8,128)(2,1)S(1)}, f32[3,256,256]{2,1,0:T(8,128)S(1)}, f32[2,128,256]{2,1,0:T(8,128)S(1)}) custom-call(s32[1]{0:T(128)} %bitcast.parity_ref, f32[64,1,768]{2,1,0:T(1,128)S(1)} %all_to_all.10.own_ref, bf16[9,256,256]{2,1,0:T(8,128)(2,1)} %constant.21.clone.bank_far), custom_call_target="tpu_custom_call" | custom-call | tf_op jit(solution)/shard_map/pallas_call | solution.py:201
  24.9 0.1 collective-permute-done.other_ref
  25.0 1.5 %shard_map.95 = f32[64,1,768]{2,1,0:T(1,128)S(1)} custom-call(s32[1]{0:T(128)} %bitcast.parity_ref, f32[64,1,768]{2,1,0:T(1,128)S(1)} %collective-permute-done.other_ref, f32[3,256,256]{2,1,0:T(8,128)S(1)} %get-tuple-element.15.front_ref, f32[2,128,256]{2,1,0:T(8,128)S(1)} %get-tuple-element.16.twist_ref, bf16[9,256,256]{2,1,0:T(8,128)(2,1)S(1)} %get-tuple-element.17.bank_ref), custom_call_target="tpu_custom_call" | custom-call | tf_op jit(solution)/shard_map/pallas_call | solution.py:201
  26.5 18.3 %all_to_all.11.moved_ref.refs_0_ = f32[64,1,768]{2,1,0:T(1,128)S(1)} all-to-all(f32[64,1,768]{2,1,0:T(1,128)S(1)} %shard_map.95), channel_id=1, replica_groups={{200,72,204,76,192,64,196,68,248,120,252,124,240,112,244,116,168,40,172..., dimensions={0} | all-to-all | bytes 393216 | tf_op jit(solution)/shard_map/all_to_all | solution.py:223
  44.8 0.1 collective-permute-start.1
  44.9 0.7 %shard_map.96 = (bf16[64,256]{1,0:T(8,128)(2,1)}, bf16[64,256]{1,0:T(8,128)(2,1)}, bf16[64,256]{1,0:T(8,128)(2,1)}) custom-call(f32[64,1,768]{2,1,0:T(1,128)S(1)} %all_to_all.11.moved_ref.refs_0_, bf16[64,256]{1,0:T(8,128)(2,1)S(1)} %get-tuple-element.18.key_ref, bf16[64,256]{1,0:T(8,128)(2,1)S(1)} %get-tuple-element.19.value_ref, ...), custom_call_target="tpu_custom_call" | custom-call | tf_op jit(solution)/shard_map/pallas_call | solution.py:201
  45.6 2.9 %collective-permute-done.1.right_ref = f32[1,256]{1,0:T(1,128)S(1)} collective-permute-done((f32[1,256]{1,0:T(1,128)S(1)}, f32[1,256]{1,0:T(1,128)S(1)}, u32[]{:S(2)}, u32[]{:S(2)}) %collective-permute-start.1) | collective-permute-done | bytes 1056 | tf_op jit(solution)/shard_map/ppermute | solution.py:262
  48.5 0.6 %shard_map.98 = f32[1,256]{1,0:T(1,128)} custom-call(f32[1,256]{1,0:T(1,128)S(1)} %shard_map.97.left_ref, f32[1,256]{1,0:T(1,128)S(1)} %collective-permute-done.1.right_ref), custom_call_target="tpu_custom_call" | custom-call | tf_op jit(solution)/shard_map/pallas_call | solution.py:201
  (1 shorter events, 0.0 us)
Async XLA Ops:
  23.6 1.4 %collective-permute-start = (f32[64,1,768]{2,1,0:T(1,128)S(1)}, f32[64,1,768]{2,1,0:T(1,128)S(1)}, u32[]{:S(2)}, u32[]{:S(2)}) collective-permute-start(f32[64,1,768]{2,1,0:T(1,128)S(1)} %all_to_all.10.own_ref), channel_id=1, source_target_pairs={{0,2},{2,0},{4,6},{6,4},{8,10},{10,8},{12,14},{14,12},{16,18},{18,... | collective-permute-start | bytes 589832 | tf_op jit(solution)/shard_map/ppermute | solution.py:245
  44.8 3.7 %collective-permute-start.1 = (f32[1,256]{1,0:T(1,128)S(1)}, f32[1,256]{1,0:T(1,128)S(1)}, u32[]{:S(2)}, u32[]{:S(2)}) collective-permute-start(f32[1,256]{1,0:T(1,128)S(1)} %shard_map.97.left_ref), channel_id=1, source_target_pairs={{0,1},{1,0},{2,3},{3,2},{4,5},{5,4},{6,7},{7,6},{8,9},{9,8},{10,11... | collective-permute-start | bytes 3080 | tf_op jit(solution)/shard_map/ppermute | solution.py:262
